TPU v7x, 128 devices: a whole 4x4x4 slice. The times are simulated.
128 devices in a mesh: gx: 16 (over y, z), gy: 8 (over x, core).
Axes of the slice: x: 4, y: 4, z: 4, core: 2. Of those that a mesh axis runs over, the one named last changes fastest.
Arguments:
- old_fields: float32 [18, 1024, 1024], P(None, 'gx', 'gy'), may hold values from -6 to 6
- send_block: int32 [128, 256], P(('gx', 'gy')), may hold values from -1 to 63, as said below
- pair_slot: int32 [128, 112], P(('gx', 'gy')), may hold values from 0 to 255, as said below
- pair_block: int32 [128, 112], P(('gx', 'gy')), may hold values from 0 to 63, as said below
- crossing: bfloat16 [128, 112, 3, 128, 128], P(('gx', 'gy')), as said below
- kappa: float32 [18], replicated, may hold values from 0.2 to 2
Outputs:
- new_fields: float32 [18, 1024, 1024], P(None, 'gx', 'gy')
- flux_residual: float32 [18, 1024, 1024], P(None, 'gx', 'gy')
Inputs may be any that keep to these rules, and one draw needn't show every extreme that they name: `send_block`: entry d * 2 + c of row s is the old row that device s sends in slot c to device d, or -1 where the slot is empty; every slot named by pair_slot is filled, all others are -1. `pair_slot`: in each row the entries are distinct; entry e names source e // 2; each device receives from some one source all 2 of its slots. `pair_block`: every new block of a device is named by at least one of its pairs. `crossing`: volumes are positive.
All inputs are finite; a program needn't handle non-finite values.
Results may differ from a plain program's by a relative error of at most 0.0029.
Values may be sent and summed in bfloat16 or wider, within the bound.
A program may use at most 128 MiB of HBM per device.

v0:
```python
import jax
import jax.numpy as jnp
from jax import lax
from jax.sharding import PartitionSpec as P


def with_halo(cells, sides, width):
    for axis, dim in sides:
        count = lax.axis_size(axis)
        ends = count - 1
        head = lax.slice_in_dim(cells, 0, width, axis=dim)
        tail = lax.slice_in_dim(cells, cells.shape[dim] - width, cells.shape[dim], axis=dim)
        cells = jnp.concatenate(
            [
                lax.ppermute(tail, axis, [(i, (i + 1) % count) for i in range(ends)]),
                cells,
                lax.ppermute(head, axis, [((i + 1) % count, i) for i in range(ends)]),
            ],
            axis=dim,
        )
    return cells


def minmod(first, second):
    same = first * second > 0.0
    least = jnp.minimum(jnp.abs(first), jnp.abs(second))
    return jnp.where(same, jnp.sign(first) * least, jnp.zeros_like(first))


def neighbours(extended, values):
    first_x = lax.axis_index("gx") == 0
    last_x = lax.axis_index("gx") == lax.axis_size("gx") - 1
    first_y = lax.axis_index("gy") == 0
    last_y = lax.axis_index("gy") == lax.axis_size("gy") - 1
    northern = jnp.where(first_x, values[:, :1, :], extended[:, :1, 1:-1])
    southern = jnp.where(last_x, values[:, -1:, :], extended[:, -1:, 1:-1])
    western = jnp.where(first_y, values[:, :, :1], extended[:, 1:-1, :1])
    eastern = jnp.where(last_y, values[:, :, -1:], extended[:, 1:-1, -1:])
    upper_row = jnp.concatenate([northern, values[:, :-1, :]], 1)
    lower_row = jnp.concatenate([values[:, 1:, :], southern], 1)
    left_col = jnp.concatenate([western, values[:, :, :-1]], 2)
    right_col = jnp.concatenate([values[:, :, 1:], eastern], 2)
    return (upper_row, lower_row, left_col, right_col)


def shards(old_fields, send_block, pair_slot, pair_block, crossing, kappa):
    field_count, row_count, width = old_fields.shape
    extended = with_halo(old_fields, (("gx", 1), ("gy", 2)), 1)
    upper_row, lower_row, left_col, right_col = neighbours(extended, old_fields)
    grad_x = minmod(lower_row - old_fields, old_fields - upper_row)
    grad_y = minmod(right_col - old_fields, old_fields - left_col)
    stacked = jnp.concatenate([old_fields, grad_x, grad_y], 0).astype(jnp.bfloat16)
    old_data = stacked.transpose(1, 0, 2)
    wanted = send_block[0]
    count_x = lax.axis_size("gx")
    count_y = lax.axis_size("gy")
    devices = count_x * count_y
    capacity = wanted.shape[0] // devices
    picked = jnp.take(old_data, jnp.maximum(wanted, 0), axis=0)
    outgoing = jnp.where((wanted >= 0)[:, None, None], picked, jnp.zeros_like(picked))
    incoming = lax.all_to_all(
        outgoing.reshape(devices, capacity, 3 * field_count, width),
        ("gx", "gy"),
        split_axis=0,
        concat_axis=0,
        tiled=True,
    )
    incoming = incoming.reshape(devices * capacity, 3 * field_count, width)
    pair_data = jnp.take(incoming, pair_slot[0], axis=0)
    pair_count = pair_data.shape[0]
    weights = crossing[0]
    split_data = pair_data.reshape(pair_count, 3, field_count, width)
    contrib = jnp.einsum(
        "pfo,pon->pfn", split_data[:, 0], weights[:, 0], preferred_element_type=jnp.float32
    )
    contrib = contrib + jnp.einsum(
        "pfo,pon->pfn", split_data[:, 1], weights[:, 1], preferred_element_type=jnp.float32
    )
    contrib = contrib + jnp.einsum(
        "pfo,pon->pfn", split_data[:, 2], weights[:, 2], preferred_element_type=jnp.float32
    )
    selector = (pair_block[0][None, :] == jnp.arange(row_count, dtype=jnp.int32)[:, None]).astype(
        jnp.float32
    )
    remapped = jnp.einsum("bp,pfn->bfn", selector, contrib, precision=lax.Precision.HIGHEST)
    col_sums = jnp.sum(weights[:, 0], axis=1, dtype=jnp.float32)
    volume = jnp.dot(selector, col_sums, precision=lax.Precision.HIGHEST)
    new_fields = (remapped / volume[:, None, :]).transpose(1, 0, 2)
    extended_new = with_halo(new_fields.astype(jnp.bfloat16), (("gx", 1), ("gy", 2)), 1).astype(
        new_fields.dtype
    )
    upper_row, lower_row, left_col, right_col = neighbours(extended_new, new_fields)
    laplace = upper_row + lower_row + left_col + right_col - 4.0 * new_fields
    return (new_fields, kappa[:, None, None] * laplace)


def solution(mesh):
    placed = (
        P(None, "gx", "gy"),
        P(("gx", "gy"), None),
        P(("gx", "gy"), None),
        P(("gx", "gy"), None),
        P(("gx", "gy"), None, None, None, None),
        P(),
    )
    return jax.shard_map(
        shards,
        mesh=mesh,
        in_specs=placed,
        out_specs=(P(None, "gx", "gy"), P(None, "gx", "gy")),
        check_vma=False,
    )
```

profile of v0, /device:TPU:1, one launch (start us, length us, event | category | flops | bytes accessed | tf_op | source)
XLA Modules:
  0.0 133.2 jit_solution(2724754713062741562)
XLA Ops:
  0.6 1.6 %fusion.22 = (f32[18,1,128]{2,1,0:T(1,128)S(1)}, f32[18,1,128]{2,1,0:T(1,128)}) fusion(f32[18,64,128]{2,1,0:T(8,128)} %param.6), kind=kLoop, calls=%fused_computation.70 | loop fusion | bytes 36864 | tf_op jit(solution)/shard_map/slice | solution.py:36
  2.2 5.0 %collective-permute-start.1 = (f32[18,1,128]{2,1,0:T(1,128)S(1)}, f32[18,1,128]{2,1,0:T(1,128)}, u32[]{:S(2)}, u32[]{:S(2)}) collective-permute-start(f32[18,1,128]{2,1,0:T(1,128)S(1)} %get-tuple-element.25), channel_id=1, source_target_pairs={{0,8},{8,16},{16,24},{24,32},{32,40},{40,48},{48,56},{56,64},{64,7... | collective-permute-start | bytes 27656 | tf_op jit(solution)/shard_map/ppermute | solution.py:15
  7.2 1.4 %collective-permute-start = (f32[18,1,128]{2,1,0:T(1,128)}, f32[18,1,128]{2,1,0:T(1,128)}, u32[]{:S(2)}, u32[]{:S(2)}) collective-permute-start(f32[18,1,128]{2,1,0:T(1,128)} %get-tuple-element.26), channel_id=1, source_target_pairs={{8,0},{16,8},{24,16},{32,24},{40,32},{48,40},{56,48},{64,56},{72,6... | collective-permute-start | bytes 27656 | tf_op jit(solution)/shard_map/ppermute | solution.py:17
  8.6 2.3 %fusion.20 = (f32[18,63,128]{2,1,0:T(8,128)S(1)}, f32[18,63,128]{2,1,0:T(8,128)}) fusion(f32[18,64,128]{2,1,0:T(8,128)} %param.6), kind=kLoop, calls=%fused_computation.68 | loop fusion | bytes 2322432 | tf_op jit(solution)/shard_map/slice | solution.py:40
  15.1 2.1 %copy.64 = f32[18,1,128]{1,2,0:T(8,128)} copy(f32[18,1,128]{2,1,0:T(1,128)} %collective-permute-done) | data formatting | bytes 18432 | tf_op jit(solution)/shard_map/ppermute | solution.py:17
  17.2 1.7 %pad_maximum_fusion.7 = (f32[18,66,1]{1,2,0:T(1,128)S(1)}, f32[18,66,1]{1,2,0:T(1,128)}) fusion(f32[18,1,128]{1,2,0:T(8,128)} %copy.64, f32[18,64,128]{1,2,0:T(8,128)S(1)} %copy.63, f32[18,1,128]{1,2,0:T(8,128)S(1)} %copy.62), kind=kLoop, calls=%fused_computation.55 | loop fusion | flops 4752 | bytes 617760 | tf_op jit(solution)/shard_map/slice | solution.py:11
  18.9 2.9 %collective-permute-start.2 = (f32[18,66,1]{1,2,0:T(1,128)S(1)}, f32[18,66,1]{1,2,0:T(1,128)S(1)}, u32[]{:S(2)}, u32[]{:S(2)}) collective-permute-start(f32[18,66,1]{1,2,0:T(1,128)S(1)} %get-tuple-element.4), channel_id=1, source_target_pairs={{1,0},{2,1},{3,2},{4,3},{5,4},{6,5},{7,6},{9,8},{10,9},{11,10},{12... | collective-permute-start | bytes 14264 | tf_op jit(solution)/shard_map/ppermute | solution.py:17
  21.7 3.0 %collective-permute-start.3 = (f32[18,66,1]{1,2,0:T(1,128)}, f32[18,66,1]{1,2,0:T(1,128)S(1)}, u32[]{:S(2)}, u32[]{:S(2)}) collective-permute-start(f32[18,66,1]{1,2,0:T(1,128)} %get-tuple-element.5), channel_id=1, source_target_pairs={{0,1},{1,2},{2,3},{3,4},{4,5},{5,6},{6,7},{8,9},{9,10},{10,11},{11... | collective-permute-start | bytes 14264 | tf_op jit(solution)/shard_map/ppermute | solution.py:15
  24.7 1.3 broadcast_select_fusion.5
  28.5 1.5 %slice_select_fusion.2 = (f32[18,64,1]{2,1,0:T(8,128)S(1)}, f32[18,64,1]{2,1,0:T(8,128)S(1)}) fusion(f32[18,64,1]{2,1,0:T(8,128)} %copy.65, f32[18,64,128]{2,1,0:T(8,128)S(1)} %copy-done.2, pred[]{:T(512)S(6)} %eq.37, f32[18,64,1]{2,1,0:T(8,128)} %copy.66, pred[]{:T(512)S(6)} %eq.38), kind=kLoop, calls=%fused_computation.36 | loop fusion | flops 2304 | bytes 27650 | tf_op jit(solution)/shard_map/jit(_where)/select_n | solution.py:38
  31.7 3.1 %gather_fusion = bf16[256,54,128]{2,1,0:T(8,128)(2,1)} fusion(bf16[64,54,128]{2,1,0:T(8,128)(2,1)S(1)} %copy.67, s32[1024]{0:T(1024)} %pad_clamp_fusion.1), kind=kCustom, calls=%fused_computation | custom fusion | bytes 7078912 | tf_op jit(solution)/shard_map/jit(_take)/gather | solution.py:59
  34.8 8.3 %broadcast_select_fusion.1 = bf16[128,2,54,128]{3,1,2,0:T(2,128)(2,1)} fusion(pred[128,2]{1,0:T(8,128)(4,1)S(1)} %ge.28, pred[128,2]{1,0:T(8,128)(4,1)S(1)} %copy-done.7, bf16[128,2,54,128]{3,2,1,0:T(8,128)(2,1)} %bitcast.52), kind=kLoop, calls=%fused_computation.5 | loop fusion | flops 3538944 | bytes 7078400 | tf_op jit(solution)/shard_map/jit(_where)/select_n | solution.py:60
  43.1 10.3 %all-to-all-start = ((bf16[128,2,54,128]{3,1,2,0:T(2,128)(2,1)}), bf16[128,2,54,128]{3,1,2,0:T(2,128)(2,1)S(1)}, u32[]{:S(2)}, u32[]{:S(2)}) async-start(bf16[128,2,54,128]{3,1,2,0:T(2,128)(2,1)} %broadcast_select_fusion.1), calls=%async_computation | async-start | bytes 7077888 | tf_op jit(solution)/shard_map/all_to_all | solution.py:61
  53.4 6.1 %copy.81 = bf16[1,112,3,128,128]{4,3,1,2,0:T(8,128)(2,1)S(1)} copy(bf16[1,112,3,128,128]{4,3,2,1,0:T(8,128)(2,1)} %param.10) | data formatting | bytes 22020096 | tf_op args[4]
  59.6 4.1 %copy-done = bf16[1,112,3,128,128]{4,3,1,2,0:T(8,128)(2,1)} copy-done((bf16[1,112,3,128,128]{4,3,1,2,0:T(8,128)(2,1)}, bf16[1,112,3,128,128]{4,3,1,2,0:T(8,128)(2,1)S(1)}, u32[]{:S(2)}) %copy-start) | copy-done | bytes 11010072
  65.6 33.8 %all-to-all-done = bf16[128,2,54,128]{3,1,2,0:T(2,128)(2,1)S(1)} async-done(((bf16[128,2,54,128]{3,1,2,0:T(2,128)(2,1)}), bf16[128,2,54,128]{3,1,2,0:T(2,128)(2,1)S(1)}, u32[]{:S(2)}, u32[]{:S(2)}) %all-to-all-start) | async-done | bytes 3538976 | tf_op jit(solution)/shard_map/all_to_all | solution.py:61
  99.4 2.5 %copy.69 = bf16[128,2,54,128]{3,2,1,0:T(8,128)(2,1)} copy(bf16[128,2,54,128]{3,1,2,0:T(2,128)(2,1)S(1)} %all-to-all-done) | data formatting | bytes 7077888 | tf_op jit(solution)/shard_map/all_to_all | solution.py:61
  101.9 3.0 %gather_fusion.1 = bf16[112,54,128]{2,1,0:T(8,128)(2,1)S(1)} fusion(bf16[256,54,128]{2,1,0:T(8,128)(2,1)} %bitcast.53, s32[1024]{0:T(1024)S(1)} %pad_clamp_fusion), kind=kCustom, calls=%fused_computation.1 | custom fusion | bytes 3097024 | tf_op jit(solution)/shard_map/jit(_take)/gather | solution.py:69
  105.5 3.4 %fusion.1 = f32[112,18,128]{2,1,0:T(8,128)S(1)} fusion(bf16[112,3,128,128]{3,2,0,1:T(8,128)(2,1)} %bitcast.49, bf16[112,3,18,128]{3,2,0,1:T(8,128)(2,1)S(1)} %copy_select_fusion), kind=kOutput, calls=%fused_computation.9 | convolution fusion | flops 66060288 | bytes 5390336 | tf_op jit(solution)/shard_map/pfo,pon->pfn/dot_general | solution.py:76
  115.7 2.9 %collective-permute-done.5 = bf16[18,1,128]{2,1,0:T(2,128)(2,1)S(1)} collective-permute-done((bf16[18,1,128]{2,1,0:T(2,128)(2,1)S(1)}, bf16[18,1,128]{2,1,0:T(2,128)(2,1)S(1)}, u32[]{:S(2)}, u32[]{:S(2)}) %collective-permute-start.5) | collective-permute-done | bytes 4640 | tf_op jit(solution)/shard_map/ppermute | solution.py:17
  118.9 4.1 %collective-permute-start.6 = (bf16[18,66,1]{2,1,0:T(8,128)(2,1)S(1)}, bf16[18,66,1]{2,1,0:T(8,128)(2,1)S(1)}, u32[]{:S(2)}, u32[]{:S(2)}) collective-permute-start(bf16[18,66,1]{2,1,0:T(8,128)(2,1)S(1)} %get-tuple-element.27), channel_id=1, source_target_pairs={{0,1},{1,2},{2,3},{3,4},{4,5},{5,6},{6,7},{8,9},{9,10},{10,11},{11... | collective-permute-start | bytes 7136 | tf_op jit(solution)/shard_map/ppermute | solution.py:15
  123.0 2.2 %collective-permute-start.7 = (bf16[18,66,1]{2,1,0:T(8,128)(2,1)S(1)}, bf16[18,66,1]{2,1,0:T(8,128)(2,1)S(1)}, u32[]{:S(2)}, u32[]{:S(2)}) collective-permute-start(bf16[18,66,1]{2,1,0:T(8,128)(2,1)S(1)} %get-tuple-element.28), channel_id=1, source_target_pairs={{1,0},{2,1},{3,2},{4,3},{5,4},{6,5},{7,6},{9,8},{10,9},{11,10},{12... | collective-permute-start | bytes 7136 | tf_op jit(solution)/shard_map/ppermute | solution.py:17
  125.4 1.7 %collective-permute-done.6 = bf16[18,66,1]{2,1,0:T(8,128)(2,1)S(1)} collective-permute-done((bf16[18,66,1]{2,1,0:T(8,128)(2,1)S(1)}, bf16[18,66,1]{2,1,0:T(8,128)(2,1)S(1)}, u32[]{:S(2)}, u32[]{:S(2)}) %collective-permute-start.6) | collective-permute-done | bytes 2408 | tf_op jit(solution)/shard_map/ppermute | solution.py:15
  127.1 4.4 %collective-permute-done.7 = bf16[18,66,1]{2,1,0:T(8,128)(2,1)S(1)} collective-permute-done((bf16[18,66,1]{2,1,0:T(8,128)(2,1)S(1)}, bf16[18,66,1]{2,1,0:T(8,128)(2,1)S(1)}, u32[]{:S(2)}, u32[]{:S(2)}) %collective-permute-start.7) | collective-permute-done | bytes 2408 | tf_op jit(solution)/shard_map/ppermute | solution.py:17
  (69 shorter events, 19.6 us)
Async XLA Ops:
  0.6 10.2 %copy-start.2 = (f32[18,64,128]{2,1,0:T(8,128)S(1)}, f32[18,64,128]{2,1,0:T(8,128)}, u32[]{:S(2)}) copy-start(f32[18,64,128]{2,1,0:T(8,128)} %param.6) | copy-start | bytes 1769476
  2.2 11.7 %collective-permute-start.1 = (f32[18,1,128]{2,1,0:T(1,128)S(1)}, f32[18,1,128]{2,1,0:T(1,128)}, u32[]{:S(2)}, u32[]{:S(2)}) collective-permute-start(f32[18,1,128]{2,1,0:T(1,128)S(1)} %get-tuple-element.25), channel_id=1, source_target_pairs={{0,8},{8,16},{16,24},{24,32},{32,40},{40,48},{48,56},{56,64},{64,7... | collective-permute-start | bytes 27656 | tf_op jit(solution)/shard_map/ppermute | solution.py:15
  7.2 4.9 %copy-start.11 = (s32[1,256]{1,0:T(1,128)S(1)}, s32[1,256]{1,0:T(1,128)}, u32[]{:S(2)}) copy-start(s32[1,256]{1,0:T(1,128)} %param.7) | copy-start | bytes 3076
  7.2 7.9 %collective-permute-start = (f32[18,1,128]{2,1,0:T(1,128)}, f32[18,1,128]{2,1,0:T(1,128)}, u32[]{:S(2)}, u32[]{:S(2)}) collective-permute-start(f32[18,1,128]{2,1,0:T(1,128)} %get-tuple-element.26), channel_id=1, source_target_pairs={{8,0},{16,8},{24,16},{32,24},{40,32},{48,40},{56,48},{64,56},{72,6... | collective-permute-start | bytes 27656 | tf_op jit(solution)/shard_map/ppermute | solution.py:17
  18.9 7.2 %collective-permute-start.2 = (f32[18,66,1]{1,2,0:T(1,128)S(1)}, f32[18,66,1]{1,2,0:T(1,128)S(1)}, u32[]{:S(2)}, u32[]{:S(2)}) collective-permute-start(f32[18,66,1]{1,2,0:T(1,128)S(1)} %get-tuple-element.4), channel_id=1, source_target_pairs={{1,0},{2,1},{3,2},{4,3},{5,4},{6,5},{7,6},{9,8},{10,9},{11,10},{12... | collective-permute-start | bytes 14264 | tf_op jit(solution)/shard_map/ppermute | solution.py:17
  21.7 5.5 %collective-permute-start.3 = (f32[18,66,1]{1,2,0:T(1,128)}, f32[18,66,1]{1,2,0:T(1,128)S(1)}, u32[]{:S(2)}, u32[]{:S(2)}) collective-permute-start(f32[18,66,1]{1,2,0:T(1,128)} %get-tuple-element.5), channel_id=1, source_target_pairs={{0,1},{1,2},{2,3},{3,4},{4,5},{5,6},{6,7},{8,9},{9,10},{10,11},{11... | collective-permute-start | bytes 14264 | tf_op jit(solution)/shard_map/ppermute | solution.py:15
  27.3 2.7 %copy-start.4 = (f32[18,63,128]{2,1,0:T(8,128)S(1)}, f32[18,63,128]{2,1,0:T(8,128)}, u32[]{:S(2)}) copy-start(f32[18,63,128]{2,1,0:T(8,128)} %get-tuple-element.18) | copy-start | bytes 1741828
  27.3 2.6 %copy-start.5 = (f32[18,64,127]{2,1,0:T(8,128)S(1)}, f32[18,64,127]{2,1,0:T(8,128)}, u32[]{:S(2)}) copy-start(f32[18,64,127]{2,1,0:T(8,128)} %get-tuple-element.21) | copy-start | bytes 1755652
  27.4 2.6 %copy-start.6 = (f32[18,64,127]{2,1,0:T(8,128)S(1)}, f32[18,64,127]{2,1,0:T(8,128)}, u32[]{:S(2)}) copy-start(f32[18,64,127]{2,1,0:T(8,128)} %get-tuple-element.22) | copy-start | bytes 1755652
  28.5 1.5 %copy-start.8 = (f32[18,1,128]{2,1,0:T(1,128)S(1)}, f32[18,1,128]{2,1,0:T(1,128)}, u32[]{:S(2)}) copy-start(f32[18,1,128]{2,1,0:T(1,128)} %get-tuple-element.19) | copy-start | bytes 27652
  28.5 1.6 %copy-start.9 = (f32[18,1,128]{2,1,0:T(1,128)S(1)}, f32[18,1,128]{2,1,0:T(1,128)}, u32[]{:S(2)}) copy-start(f32[18,1,128]{2,1,0:T(1,128)} %get-tuple-element.20) | copy-start | bytes 27652
  31.7 3.1 %copy-start.7 = (pred[128,2]{1,0:T(8,128)(4,1)S(1)}, pred[128,2]{1,0:T(8,128)(4,1)}, u32[]{:S(2)}) copy-start(pred[128,2]{1,0:T(8,128)(4,1)} %le.30) | copy-start | bytes 772
  43.1 56.3 %all-to-all-start = ((bf16[128,2,54,128]{3,1,2,0:T(2,128)(2,1)}), bf16[128,2,54,128]{3,1,2,0:T(2,128)(2,1)S(1)}, u32[]{:S(2)}, u32[]{:S(2)}) async-start(bf16[128,2,54,128]{3,1,2,0:T(2,128)(2,1)} %broadcast_select_fusion.1), calls=%async_computation | async-start | bytes 7077888 | tf_op jit(solution)/shard_map/all_to_all | solution.py:61
  53.4 6.1 %copy-start.14 = (s32[1,112]{1,0:T(1,128)S(1)}, s32[1,112]{1,0:T(1,128)}, u32[]{:S(2)}) copy-start(s32[1,112]{1,0:T(1,128)} %param.8) | copy-start | bytes 1348
  59.5 4.2 %copy-start = (bf16[1,112,3,128,128]{4,3,1,2,0:T(8,128)(2,1)}, bf16[1,112,3,128,128]{4,3,1,2,0:T(8,128)(2,1)S(1)}, u32[]{:S(2)}) copy-start(bf16[1,112,3,128,128]{4,3,1,2,0:T(8,128)(2,1)S(1)} %copy.81) | copy-start | bytes 33030148
  59.5 5.3 %copy-start.12 = (s32[1,112]{1,0:T(1,128)S(1)}, s32[1,112]{1,0:T(1,128)}, u32[]{:S(2)}) copy-start(s32[1,112]{1,0:T(1,128)} %param.9) | copy-start | bytes 1348
  104.9 5.2 %copy-start.1 = (bf16[1,112,3,128,128]{4,3,1,2,0:T(8,128)(2,1)S(1)}, bf16[1,112,3,128,128]{4,3,1,2,0:T(8,128)(2,1)}, u32[]{:S(2)}) copy-start(bf16[1,112,3,128,128]{4,3,1,2,0:T(8,128)(2,1)} %copy-done) | copy-start | bytes 33030148
  111.2 1.1 copy-start.10
  112.9 19.0 %copy-start.3 = (f32[18,64,128]{2,1,0:T(8,128)}, f32[18,64,128]{2,1,0:T(8,128)S(1)}, u32[]{:S(2)}) copy-start(f32[18,64,128]{2,1,0:T(8,128)S(1)} %get-tuple-element.32) | copy-start | bytes 1769476
  112.9 2.8 %collective-permute-start.4 = (bf16[18,1,128]{2,1,0:T(2,128)(2,1)S(1)}, bf16[18,1,128]{2,1,0:T(2,128)(2,1)S(1)}, u32[]{:S(2)}, u32[]{:S(2)}) collective-permute-start(bf16[18,1,128]{2,1,0:T(2,128)(2,1)S(1)} %get-tuple-element.29), channel_id=1, source_target_pairs={{0,8},{8,16},{16,24},{24,32},{32,40},{40,48},{48,56},{56,64},{64,7... | collective-permute-start | bytes 13832 | tf_op jit(solution)/shard_map/ppermute | solution.py:15
  114.2 4.4 %collective-permute-start.5 = (bf16[18,1,128]{2,1,0:T(2,128)(2,1)S(1)}, bf16[18,1,128]{2,1,0:T(2,128)(2,1)S(1)}, u32[]{:S(2)}, u32[]{:S(2)}) collective-permute-start(bf16[18,1,128]{2,1,0:T(2,128)(2,1)S(1)} %get-tuple-element.30), channel_id=1, source_target_pairs={{8,0},{16,8},{24,16},{32,24},{40,32},{48,40},{56,48},{64,56},{72,6... | collective-permute-start | bytes 13832 | tf_op jit(solution)/shard_map/ppermute | solution.py:17
  118.9 8.2 %collective-permute-start.6 = (bf16[18,66,1]{2,1,0:T(8,128)(2,1)S(1)}, bf16[18,66,1]{2,1,0:T(8,128)(2,1)S(1)}, u32[]{:S(2)}, u32[]{:S(2)}) collective-permute-start(bf16[18,66,1]{2,1,0:T(8,128)(2,1)S(1)} %get-tuple-element.27), channel_id=1, source_target_pairs={{0,1},{1,2},{2,3},{3,4},{4,5},{5,6},{6,7},{8,9},{9,10},{10,11},{11... | collective-permute-start | bytes 7136 | tf_op jit(solution)/shard_map/ppermute | solution.py:15
  123.0 8.4 %collective-permute-start.7 = (bf16[18,66,1]{2,1,0:T(8,128)(2,1)S(1)}, bf16[18,66,1]{2,1,0:T(8,128)(2,1)S(1)}, u32[]{:S(2)}, u32[]{:S(2)}) collective-permute-start(bf16[18,66,1]{2,1,0:T(8,128)(2,1)S(1)} %get-tuple-element.28), channel_id=1, source_target_pairs={{1,0},{2,1},{3,2},{4,3},{5,4},{6,5},{7,6},{9,8},{10,9},{11,10},{12... | collective-permute-start | bytes 7136 | tf_op jit(solution)/shard_map/ppermute | solution.py:17
  125.4 6.6 %copy-start.13 = (f32[18]{0:T(128)S(1)}, f32[18]{0:T(128)}, u32[]{:S(2)}) copy-start(f32[18]{0:T(128)} %param.11) | copy-start | bytes 220
where the time goes:
time: 134 us; the launch traced here: 133 us
  waiting for transfers between devices  42.8 us (32%)
  local copies, waits for them, and re-layouts  33.2 us (25%)
  starting transfers between devices  31.4 us (23%)
  other arithmetic  17.8 us (13%)
  matrix products  6.91 us (5%)
    all_to_all x1, waiting for transfers between devices, shards(): lax.all_to_all(outgoing.reshape(devices, capacity, 3 * field_count, width...  33.8 us
    ppermute x4, starting transfers between devices, with_halo(): lax.ppermute(tail, axis, [(i, (i + 1) % count) for i in range(ends)])  13.4 us
    unnamed x32, local copies, waits for them, and re-layouts  11.9 us
    all_to_all x1, starting transfers between devices, shards(): lax.all_to_all(outgoing.reshape(devices, capacity, 3 * field_count, width...  10.3 us
    select_n x1, other arithmetic, shards(): jnp.where((wanted >= 0)[:, None, None], picked, jnp.zeros_like(picked))  8.32 us
    ppermute x4, starting transfers between devices, with_halo(): lax.ppermute(head, axis, [((i + 1) % count, i) for i in range(ends)])  7.77 us
    ppermute x4, waiting for transfers between devices, with_halo(): lax.ppermute(head, axis, [((i + 1) % count, i) for i in range(ends)])  7.28 us
    dot_general x1, matrix products, shards(): jnp.einsum('pfo,pon->pfn', split_data[:, 1], weights[:, 1], preferred_ele...  3.38 us
  transfers between devices with their start and end apart: 9, of which 4 were waited for; matrix products, arithmetic and copies ran while one was open for 13% of the time, Pallas kernels for 0%

commit v1 on v0

v1 whole, which is shorter than its diff:
```python
import functools

import jax
import jax.numpy as jnp
from jax import lax
from jax.experimental import pallas as pl
from jax.experimental.pallas import tpu as pltpu
from jax.sharding import PartitionSpec as P

MESH = pl.DeviceIdType.MESH
F32 = jnp.float32
BF16 = jnp.bfloat16

FIELDS = 18
FULL = 16
ROWS = 64
LANES = 128
PAIRS = 112
CAP = 2
SLAB = 24
VOLUME = 18


def minmod(first, second):
    least = jnp.where(first > 0.0, jnp.minimum(first, second), jnp.maximum(first, second))
    return jnp.where(first * second > 0.0, least, jnp.zeros_like(first))


def iota(shape, axis):
    return lax.broadcasted_iota(jnp.int32, shape, axis)


def loop(count, step, body):
    def outer(n, carry):
        for part in range(step):
            body(n * step + part)
        return carry

    lax.fori_loop(0, count // step, outer, 0)


def kernel(
    nx,
    ny,
    old_hbm,
    crossing_hbm,
    wanted,
    slots,
    blocks,
    kappa,
    new_ref,
    flux_ref,
    u,
    gx,
    gy,
    rest,
    table_u,
    table_g,
    table_lo,
    table_hi,
    send_a,
    send_b,
    recv_a,
    recv_b,
    weights,
    contrib,
    row_out,
    row_in,
    col_out,
    col_in,
    row_out2,
    row_in2,
    col_out2,
    col_in2,
    local_sem,
    halo_send,
    halo_recv,
    halo_send2,
    halo_recv2,
    send_sem,
    recv_sem,
):
    i = lax.axis_index("gx")
    j = lax.axis_index("gy")
    count = nx * ny
    me = i * ny + j

    get_old = pltpu.make_async_copy(old_hbm, u.at[pl.ds(0, FIELDS * ROWS)], local_sem.at[0])
    get_old.start()
    get_weights = pltpu.make_async_copy(crossing_hbm, weights, local_sem.at[1])
    get_weights.start()

    barrier = pltpu.get_barrier_semaphore()

    def greet(k, carry):
        d = lax.rem(me + k, count)
        pl.semaphore_signal(
            barrier, inc=1, device_id=(d // ny, lax.rem(d, ny)), device_id_type=MESH
        )
        return carry

    lax.fori_loop(1, count, greet, 0)

    after_x = (lax.rem(i + 1, nx), j)
    before_x = (lax.rem(i + nx - 1, nx), j)
    after_y = (i, lax.rem(j + 1, ny))
    before_y = (i, lax.rem(j + ny - 1, ny))
    first_x, last_x = i == 0, i == nx - 1
    first_y, last_y = j == 0, j == ny - 1

    lane = iota((ROWS, LANES), 1)
    row = iota((ROWS, LANES), 0)

    def field(ref, f):
        return ref[pl.ds(f * ROWS, ROWS), :]

    zeros = jnp.zeros((ROWS, LANES), F32)
    for f in range(FIELDS, SLAB):
        u[pl.ds(f * ROWS, ROWS), :] = zeros
        gy[pl.ds(f * ROWS, ROWS), :] = zeros
    for f in range(4, 8):
        rest[pl.ds(f * ROWS, ROWS), :] = zeros
    get_old.wait()
    row_out[0] = u[pl.ds(ROWS - 1, SLAB, stride=ROWS), :]
    row_out[1] = u[pl.ds(0, SLAB, stride=ROWS), :]
    head, tail = zeros, zeros
    for f in range(FIELDS):
        cells = field(u, f)
        head = jnp.where(lane == f, pltpu.roll(cells, f, 1) if f else cells, head)
        tail = jnp.where(lane == f, pltpu.roll(cells, f + 1, 1), tail)
    col_out[0] = tail
    col_out[1] = head

    def value_row(r):
        table_u[r] = u[pl.ds(r, FULL, stride=ROWS), :].astype(BF16)

    loop(ROWS, 8, value_row)

    pl.semaphore_wait(barrier, count - 1)

    halo = []
    for n, (source, target, device) in enumerate(
        (
            (row_out.at[0], row_in.at[0], after_x),
            (row_out.at[1], row_in.at[1], before_x),
            (col_out.at[0], col_in.at[0], after_y),
            (col_out.at[1], col_in.at[1], before_y),
        )
    ):
        copy = pltpu.make_async_remote_copy(
            src_ref=source,
            dst_ref=target,
            send_sem=halo_send.at[n],
            recv_sem=halo_recv.at[n],
            device_id=device,
            device_id_type=MESH,
        )
        copy.start()
        halo.append(copy)

    y, z = i // 4, lax.rem(i, 4)
    x, c = j // 2, lax.rem(j, 2)

    def partner(k):
        kc = k // 64
        low = lax.rem(k, 64)
        kx = lax.rem(low, 4)
        ky = lax.rem(low // 4 + kx, 4)
        kz = lax.rem(low // 16 + kx + 2 * ky, 4)
        di = lax.rem(y + ky, 4) * 4 + lax.rem(z + kz, 4)
        dj = lax.rem(x + kx, 4) * 2 + lax.rem(c + kc, 2)
        return di, dj

    def row_of(d, slot):
        return jnp.maximum(wanted[0, d * CAP + slot], 0)

    def pack_a(ref, at, d):
        ref[2 * at] = table_u[row_of(d, 0)]
        ref[2 * at + 1] = table_u[row_of(d, 1)]

    def send_part_a(k, carry):
        di, dj = partner(k)
        d = di * ny + dj
        pack_a(send_a, d, d)
        pltpu.make_async_remote_copy(
            src_ref=send_a.at[pl.ds(2 * d, 2)],
            dst_ref=recv_a.at[pl.ds(2 * me, 2)],
            send_sem=send_sem.at[0],
            recv_sem=recv_sem.at[0],
            device_id=(di, dj),
            device_id_type=MESH,
        ).start()
        return carry

    lax.fori_loop(1, count, send_part_a, 0)
    pack_a(recv_a, me, me)

    for copy in halo:
        copy.wait()
    for f in range(FIELDS):
        cells = field(u, f)
        north = jnp.where(first_x, cells[0:1, :], row_in[0, f : f + 1, :])
        south = jnp.where(last_x, cells[ROWS - 1 :, :], row_in[1, f : f + 1, :])
        upper = jnp.where(row == 0, north, pltpu.roll(cells, 1, 0))
        lower = jnp.where(row == ROWS - 1, south, pltpu.roll(cells, ROWS - 1, 0))
        grad = minmod(lower - cells, cells - upper)
        gx[pl.ds(f * ROWS, ROWS), :] = grad
        west = pltpu.roll(col_in[0], LANES - f, 1) if f else col_in[0]
        east = pltpu.roll(col_in[1], LANES - 1 - f, 1)
        west = jnp.where(first_y, cells, west)
        east = jnp.where(last_y, cells, east)
        left = jnp.where(lane == 0, west, pltpu.roll(cells, 1, 1))
        right = jnp.where(lane == LANES - 1, east, pltpu.roll(cells, LANES - 1, 1))
        gy[pl.ds(f * ROWS, ROWS), :] = minmod(right - cells, cells - left)
        if f >= FULL:
            rest[pl.ds((f - FULL) * ROWS, ROWS), :] = cells
            rest[pl.ds((2 + f - FULL) * ROWS, ROWS), :] = grad

    small_lane = iota((8, LANES), 1)
    small_row = iota((8, LANES), 0)

    def gradient_row(r):
        table_g[r] = gx[pl.ds(r, FULL, stride=ROWS), :].astype(BF16)
        table_lo[r] = rest[pl.ds(r, 8, stride=ROWS), :]
        edges = pltpu.roll(gy[pl.ds(r, 8, stride=ROWS), :], 1, 1)
        middle = pltpu.roll(gy[pl.ds(8 * ROWS + r, 8, stride=ROWS), :], 3, 1)
        last = pltpu.roll(gy[pl.ds(16 * ROWS + r, 8, stride=ROWS), :], 5, 1)
        table_hi[r] = jnp.where(small_lane < 2, edges, jnp.where(small_lane < 4, middle, last))

    loop(ROWS, 8, gradient_row)

    def pack_b(ref, at, d):
        r0, r1 = row_of(d, 0), row_of(d, 1)
        ref[3 * at] = table_g[r0]
        ref[3 * at + 1] = table_g[r1]
        low = jnp.where(small_row < 4, table_lo[r0], pltpu.roll(table_lo[r1], 4, 0))
        high = jnp.where(small_lane < 64, table_hi[r0], pltpu.roll(table_hi[r1], 64, 1))
        ref[3 * at + 2] = jnp.concatenate([low, high], 0).astype(BF16)

    def send_part_b(k, carry):
        di, dj = partner(k)
        d = di * ny + dj
        pack_b(send_b, d, d)
        pltpu.make_async_remote_copy(
            src_ref=send_b.at[pl.ds(3 * d, 3)],
            dst_ref=recv_b.at[pl.ds(3 * me, 3)],
            send_sem=send_sem.at[1],
            recv_sem=recv_sem.at[1],
            device_id=(di, dj),
            device_id_type=MESH,
        ).start()
        return carry

    lax.fori_loop(1, count, send_part_b, 0)
    pack_b(recv_b, me, me)

    get_weights.wait()
    others = count - 1
    for n, (out, landed, tiles) in enumerate(((send_a, recv_a, 2), (send_b, recv_b, 3))):
        whole = pl.ds(0, tiles * others)
        pltpu.make_async_copy(landed.at[whole], landed.at[whole], recv_sem.at[n]).wait()

    def grad_y(cells, west, east):
        lanes = iota(cells.shape, 1)
        step = pltpu.roll(cells, LANES - 1, 1) - cells
        inner = minmod(step, pltpu.roll(step, 1, 1))
        return jnp.where(lanes == 0, west, jnp.where(lanes == LANES - 1, east, inner))

    def product(p):
        e = slots[0, p]
        s = e // 2
        second = lax.rem(e, 2) == 1
        values = recv_a[e]
        grads = recv_b[3 * s + lax.rem(e, 2)]
        mixed = recv_b[3 * s + 2].astype(F32)
        low, high = mixed[0:8], mixed[8:16]
        low = jnp.where(second, pltpu.roll(low, 4, 0), low)
        high = jnp.where(second, pltpu.roll(high, 64, 1), high)
        wide = values.astype(F32)
        parts = []
        for n, cells in enumerate((wide[0:8], wide[8:16], low)):
            ends = pltpu.roll(high, LANES - 1 - 2 * n, 1)
            parts.append(grad_y(cells, ends, ends))
        is_volume = small_row == VOLUME - FULL
        blank = jnp.zeros((8, LANES), F32)
        low_u = jnp.where(is_volume, jnp.ones((8, LANES), F32), low)
        low_g = jnp.where(is_volume, blank, pltpu.roll(low, 6, 0))
        low_y = jnp.where(is_volume, blank, parts[2])
        upper = jnp.concatenate(
            [values, grads, jnp.concatenate(parts[:2], 0).astype(BF16)], 1
        )
        lower = jnp.concatenate([low_u, low_g, low_y], 1).astype(BF16)
        left = jnp.concatenate([upper, lower], 0)
        contrib[pl.ds(pl.multiple_of(p * SLAB, SLAB), SLAB), :] = jnp.dot(
            left, weights[p], preferred_element_type=F32
        )

    loop(PAIRS, 4, product)

    chosen = (iota((ROWS, PAIRS), 0) == blocks[...]).astype(BF16)

    def gathered(f):
        terms = contrib[pl.ds(f, PAIRS, stride=SLAB), :]
        high = terms.astype(BF16)
        low = (terms - high.astype(F32)).astype(BF16)
        return jnp.dot(chosen, high, preferred_element_type=F32) + jnp.dot(
            chosen, low, preferred_element_type=F32
        )

    volume = gathered(VOLUME)
    head, tail = zeros, zeros
    for f in range(FIELDS):
        cells = gathered(f) / volume
        u[pl.ds(f * ROWS, ROWS), :] = cells
        head = jnp.where(lane == f, pltpu.roll(cells, f, 1) if f else cells, head)
        tail = jnp.where(lane == f, pltpu.roll(cells, f + 1, 1), tail)

    blank = jnp.zeros((8, LANES), F32)
    row_out2[0] = jnp.concatenate([u[pl.ds(ROWS - 1, SLAB, stride=ROWS), :], blank], 0).astype(BF16)
    row_out2[1] = jnp.concatenate([u[pl.ds(0, SLAB, stride=ROWS), :], blank], 0).astype(BF16)
    col_out2[0] = tail.astype(BF16)
    col_out2[1] = head.astype(BF16)
    halo = []
    for n, (source, target, device) in enumerate(
        (
            (row_out2.at[0], row_in2.at[0], after_x),
            (row_out2.at[1], row_in2.at[1], before_x),
            (col_out2.at[0], col_in2.at[0], after_y),
            (col_out2.at[1], col_in2.at[1], before_y),
        )
    ):
        copy = pltpu.make_async_remote_copy(
            src_ref=source,
            dst_ref=target,
            send_sem=halo_send2.at[n],
            recv_sem=halo_recv2.at[n],
            device_id=device,
            device_id_type=MESH,
        )
        copy.start()
        halo.append(copy)
    new_ref[...] = u[pl.ds(0, FIELDS * ROWS), :]
    for copy in halo:
        copy.wait()
    norths = row_in2[0].astype(F32)
    souths = row_in2[1].astype(F32)
    wests = col_in2[0].astype(F32)
    easts = col_in2[1].astype(F32)
    for f in range(FIELDS):
        cells = field(u, f)
        north = jnp.where(first_x, cells[0:1, :], norths[f : f + 1, :])
        south = jnp.where(last_x, cells[ROWS - 1 :, :], souths[f : f + 1, :])
        upper = jnp.where(row == 0, north, pltpu.roll(cells, 1, 0))
        lower = jnp.where(row == ROWS - 1, south, pltpu.roll(cells, ROWS - 1, 0))
        west = jnp.where(first_y, cells, pltpu.roll(wests, LANES - f, 1) if f else wests)
        east = jnp.where(last_y, cells, pltpu.roll(easts, LANES - 1 - f, 1))
        left = jnp.where(lane == 0, west, pltpu.roll(cells, 1, 1))
        right = jnp.where(lane == LANES - 1, east, pltpu.roll(cells, LANES - 1, 1))
        flux_ref[pl.ds(f * ROWS, ROWS), :] = kappa[f] * (
            upper + lower + left + right - 4.0 * cells
        )

    for n, (out, landed, tiles) in enumerate(((send_a, recv_a, 2), (send_b, recv_b, 3))):
        whole = pl.ds(0, tiles * others)
        pltpu.make_async_copy(out.at[whole], out.at[whole], send_sem.at[n]).wait()


def shards(nx, ny, old_fields, send_block, pair_slot, pair_block, crossing, kappa):
    shape = old_fields.shape
    count = nx * ny
    flat = (FIELDS * ROWS, LANES)
    padded = (SLAB * ROWS, LANES)
    any_space = pl.BlockSpec(memory_space=pl.ANY)
    smem = pl.BlockSpec(memory_space=pltpu.SMEM)
    vmem = pl.BlockSpec(memory_space=pltpu.VMEM)
    new_fields, flux = pl.pallas_call(
        functools.partial(kernel, nx, ny),
        out_shape=(jax.ShapeDtypeStruct(flat, F32), jax.ShapeDtypeStruct(flat, F32)),
        in_specs=[any_space, any_space, smem, smem, vmem, smem],
        out_specs=(vmem, vmem),
        scratch_shapes=[
            pltpu.VMEM(padded, F32),
            pltpu.VMEM(flat, F32),
            pltpu.VMEM(padded, F32),
            pltpu.VMEM((8 * ROWS, LANES), F32),
            pltpu.VMEM((ROWS, FULL, LANES), BF16),
            pltpu.VMEM((ROWS, FULL, LANES), BF16),
            pltpu.VMEM((ROWS, 8, LANES), F32),
            pltpu.VMEM((ROWS, 8, LANES), F32),
            pltpu.VMEM((2 * count, 16, LANES), BF16),
            pltpu.VMEM((3 * count, 16, LANES), BF16),
            pltpu.VMEM((2 * count, 16, LANES), BF16),
            pltpu.VMEM((3 * count, 16, LANES), BF16),
            pltpu.VMEM((PAIRS, 3 * LANES, LANES), BF16),
            pltpu.VMEM((PAIRS * SLAB, LANES), F32),
            pltpu.VMEM((2, SLAB, LANES), F32),
            pltpu.VMEM((2, SLAB, LANES), F32),
            pltpu.VMEM((2, ROWS, LANES), F32),
            pltpu.VMEM((2, ROWS, LANES), F32),
            pltpu.VMEM((2, 32, LANES), BF16),
            pltpu.VMEM((2, 32, LANES), BF16),
            pltpu.VMEM((2, ROWS, LANES), BF16),
            pltpu.VMEM((2, ROWS, LANES), BF16),
            pltpu.SemaphoreType.DMA((2,)),
            pltpu.SemaphoreType.DMA((4,)),
            pltpu.SemaphoreType.DMA((4,)),
            pltpu.SemaphoreType.DMA((4,)),
            pltpu.SemaphoreType.DMA((4,)),
            pltpu.SemaphoreType.DMA((2,)),
            pltpu.SemaphoreType.DMA((2,)),
        ],
        compiler_params=pltpu.CompilerParams(
            collective_id=0, has_side_effects=True, vmem_limit_bytes=48 * 2**20
        ),
        cost_estimate=pl.CostEstimate(
            flops=2 * PAIRS * 3 * LANES * LANES * SLAB,
            bytes_accessed=12 * 2**20,
            transcendentals=0,
        ),
    )(
        old_fields.reshape(flat),
        crossing.reshape(PAIRS, 3 * LANES, LANES),
        send_block,
        pair_slot,
        pair_block,
        kappa,
    )
    return new_fields.reshape(shape), flux.reshape(shape)


def solution(mesh):
    placed = (
        P(None, "gx", "gy"),
        P(("gx", "gy"), None),
        P(("gx", "gy"), None),
        P(("gx", "gy"), None),
        P(("gx", "gy"), None, None, None, None),
        P(),
    )
    return jax.shard_map(
        functools.partial(shards, mesh.shape["gx"], mesh.shape["gy"]),
        mesh=mesh,
        in_specs=placed,
        out_specs=(P(None, "gx", "gy"), P(None, "gx", "gy")),
        check_vma=False,
    )
```

time: 134 us -> 65.1 us (0.49)
  Pallas kernels: 0 us -> 58.9 us
  waiting for transfers between devices: 42.8 us -> 0 us
  starting transfers between devices: 31.4 us -> 0 us
  local copies, waits for them, and re-layouts: 33.2 us -> 5.33 us
  other arithmetic: 17.8 us -> 0 us
  matrix products: 6.91 us -> 0 us
    pallas_call x0 -> x1, Pallas kernels: none -> 58.9 us  [shards(): pl.pallas_call(functools.partial(kernel, nx, ny), out_shape=(jax.ShapeDty...]
    all_to_all x1 -> x0, waiting for transfers between devices: 33.8 us -> none  [shards(): lax.all_to_all(outgoing.reshape(devices, capacity, 3 * field_count, width...]
    ppermute x8 -> x0, starting transfers between devices: 21.1 us -> none  [the longest x4 13.4 us: with_halo(): lax.ppermute(tail, axis, [(i, (i + 1) % count) for i in range(ends)])]
    select_n x7 -> x0, other arithmetic: 12 us -> none  [the longest x1 8.32 us: shards(): jnp.where((wanted >= 0)[:, None, None], picked, jnp.zeros_like(picked))]
    all_to_all x1 -> x0, starting transfers between devices: 10.3 us -> none  [shards(): lax.all_to_all(outgoing.reshape(devices, capacity, 3 * field_count, width...]
    ppermute x8 -> x0, waiting for transfers between devices: 8.98 us -> none  [the longest x4 7.28 us: with_halo(): lax.ppermute(head, axis, [((i + 1) % count, i) for i in range(ends)])]
    slice x11 -> x0, local copies, waits for them, and re-layouts: 7.87 us -> none  [the longest x2 2.35 us: neighbours(): lower_row = jnp.concatenate([values[:, 1:, :], southern], 1)]
    dot_general x5 -> x0, matrix products: 6.91 us -> none  [the longest x1 3.38 us: shards(): jnp.einsum('pfo,pon->pfn', split_data[:, 1], weights[:, 1], preferred_ele...]
  transfers between devices with their start and end apart: 9 -> 0, of which waited for: 4 -> 0; matrix products, arithmetic and copies ran while one was open for 13% -> 0% of each run, Pallas kernels for 0% -> 0%
where the time goes in v1:
time: 65.1 us; the launch traced here: 64.9 us
  Pallas kernels  58.9 us (90%)
  local copies, waits for them, and re-layouts  5.33 us (8%)
    pallas_call x1, Pallas kernels, shards(): pl.pallas_call(functools.partial(kernel, nx, ny), out_shape=(jax.ShapeDty...  58.9 us
    unnamed x12, local copies, waits for them, and re-layouts  5.33 us

profile of v1, /device:TPU:1, one launch (start us, length us, event | category | flops | bytes accessed | tf_op | source)
XLA Modules:
  0.0 64.9 jit_solution(1505633270005534286)
XLA Ops:
  0.6 0.0 copy-start
  0.6 1.1 %copy-done = f32[18,64,128]{2,1,0:T(8,128)S(1)} copy-done((f32[18,64,128]{2,1,0:T(8,128)S(1)}, f32[18,64,128]{2,1,0:T(8,128)}, u32[]{:S(2)}) %copy-start) | copy-done | bytes 589848
  1.7 0.0 copy-start.1
  1.7 0.7 %copy-done.1 = s32[1,256]{1,0:T(1,128)S(1)} copy-done((s32[1,256]{1,0:T(1,128)S(1)}, s32[1,256]{1,0:T(1,128)}, u32[]{:S(2)}) %copy-start.1) | copy-done | bytes 1048
  2.4 0.0 copy-start.2
  2.4 0.7 %copy-done.2 = s32[1,112]{1,0:T(1,128)S(1)} copy-done((s32[1,112]{1,0:T(1,128)S(1)}, s32[1,112]{1,0:T(1,128)}, u32[]{:S(2)}) %copy-start.2) | copy-done | bytes 472
  3.0 0.0 copy-start.3
  3.0 0.7 %copy-done.3 = s32[1,112]{1,0:T(1,128)S(1)} copy-done((s32[1,112]{1,0:T(1,128)S(1)}, s32[1,112]{1,0:T(1,128)}, u32[]{:S(2)}) %copy-start.3) | copy-done | bytes 472
  3.7 0.0 copy-start.4
  3.7 0.7 %copy-done.4 = f32[18]{0:T(128)S(1)} copy-done((f32[18]{0:T(128)S(1)}, f32[18]{0:T(128)}, u32[]{:S(2)}) %copy-start.4) | copy-done | bytes 96
  4.3 58.9 %shard_map.77 = (f32[1152,128]{1,0:T(8,128)S(1)}, f32[1152,128]{1,0:T(8,128)S(1)}) custom-call(f32[1152,128]{1,0:T(8,128)S(1)} %bitcast.4, bf16[112,384,128]{2,1,0:T(8,128)(2,1)} %bitcast.7, s32[1,256]{1,0:T(1,128)S(1)} %copy-done.1, s32[1,112]{1,0:T(1,128)S(1)} %copy-done.2, s32[1,112]{1,0:T(1,128)S(1)} %copy-done.3, f32[18]{0:T(128)S(1)} %copy-done.4), custom_call_target="tpu_custom_call" | custom-call | flops 264241152 | bytes 12582912 | tf_op jit(solution)/shard_map/pallas_call | solution.py:376
  63.2 0.8 %copy.10 = f32[18,64,128]{2,1,0:T(8,128)} copy(f32[18,64,128]{2,1,0:T(8,128)S(1)} %bitcast.6) | data formatting | bytes 1179648
  64.1 0.8 %copy.11 = f32[18,64,128]{2,1,0:T(8,128)} copy(f32[18,64,128]{2,1,0:T(8,128)S(1)} %bitcast.5) | data formatting | bytes 1179648
Async XLA Ops:
  0.6 1.1 %copy-start = (f32[18,64,128]{2,1,0:T(8,128)S(1)}, f32[18,64,128]{2,1,0:T(8,128)}, u32[]{:S(2)}) copy-start(f32[18,64,128]{2,1,0:T(8,128)} %param.6) | copy-start | bytes 1769476
  1.7 0.7 %copy-start.1 = (s32[1,256]{1,0:T(1,128)S(1)}, s32[1,256]{1,0:T(1,128)}, u32[]{:S(2)}) copy-start(s32[1,256]{1,0:T(1,128)} %wanted.1) | copy-start | bytes 3076
  2.4 0.7 %copy-start.2 = (s32[1,112]{1,0:T(1,128)S(1)}, s32[1,112]{1,0:T(1,128)}, u32[]{:S(2)}) copy-start(s32[1,112]{1,0:T(1,128)} %slots.1) | copy-start | bytes 1348
  3.0 0.7 %copy-start.3 = (s32[1,112]{1,0:T(1,128)S(1)}, s32[1,112]{1,0:T(1,128)}, u32[]{:S(2)}) copy-start(s32[1,112]{1,0:T(1,128)} %blocks.1) | copy-start | bytes 1348
  3.7 0.7 %copy-start.4 = (f32[18]{0:T(128)S(1)}, f32[18]{0:T(128)}, u32[]{:S(2)}) copy-start(f32[18]{0:T(128)} %kappa.1) | copy-start | bytes 220

commit v2 on v1

--- a/solution.py
+++ b/solution.py
@@ -17,8 +17,30 @@
 LANES = 128
 PAIRS = 112
 CAP = 2
+GROUP = 6
 SLAB = 24
 VOLUME = 18
+
+
+def chip_offsets():
+    groups, seen = [], {(0, 0, 0)}
+    for code in range(1, 64):
+        offset = (code // 16, code // 4 % 4, code % 4)
+        group = []
+        for sign in (1, -1):
+            for turn in range(3):
+                other = tuple(sign * offset[(turn + axis) % 3] % 4 for axis in range(3))
+                if other not in seen:
+                    seen.add(other)
+                    group.append(other)
+        if group:
+            groups.append(group)
+    groups.sort(key=lambda group: -sum(min(step, 4 - step) for step in group[0]))
+    codes = [kx + 4 * ky + 16 * kz for group in groups for kx, ky, kz in group]
+    return [sum(codes[n + m] * 64**m for m in range(3)) for n in range(0, len(codes), 3)]
+
+
+ORDER = chip_offsets()
 
 
 def minmod(first, second):
@@ -44,12 +66,12 @@
     ny,
     old_hbm,
     crossing_hbm,
-    wanted,
-    slots,
-    blocks,
-    kappa,
+    wanted_hbm,
+    slots_hbm,
+    blocks_hbm,
     new_ref,
-    flux_ref,
+    row_ref,
+    col_ref,
     u,
     gx,
     gy,
@@ -60,8 +82,13 @@
     table_hi,
     send_a,
     send_b,
+    send_c,
     recv_a,
     recv_b,
+    recv_c,
+    wanted,
+    slots,
+    blocks,
     weights,
     contrib,
     row_out,
@@ -87,6 +114,13 @@
 
     get_old = pltpu.make_async_copy(old_hbm, u.at[pl.ds(0, FIELDS * ROWS)], local_sem.at[0])
     get_old.start()
+    small = []
+    for n, (source, target) in enumerate(
+        ((wanted_hbm, wanted), (slots_hbm, slots), (blocks_hbm, blocks))
+    ):
+        copy = pltpu.make_async_copy(source, target, local_sem.at[2 + n])
+        copy.start()
+        small.append(copy)
     get_weights = pltpu.make_async_copy(crossing_hbm, weights, local_sem.at[1])
     get_weights.start()
 
@@ -161,15 +195,26 @@
     y, z = i // 4, lax.rem(i, 4)
     x, c = j // 2, lax.rem(j, 2)
 
-    def partner(k):
-        kc = k // 64
-        low = lax.rem(k, 64)
-        kx = lax.rem(low, 4)
-        ky = lax.rem(low // 4 + kx, 4)
-        kz = lax.rem(low // 16 + kx + 2 * ky, 4)
-        di = lax.rem(y + ky, 4) * 4 + lax.rem(z + kz, 4)
-        dj = lax.rem(x + kx, 4) * 2 + lax.rem(c + kc, 2)
-        return di, dj
+    def to_partners(body):
+        def visit(kx, ky, kz, kc):
+            di = lax.rem(y + ky, 4) * 4 + lax.rem(z + kz, 4)
+            dj = lax.rem(x + kx, 4) * 2 + lax.rem(c + kc, 2)
+            body(di * ny + dj, (di, dj))
+
+        def some(n, carry):
+            kc = n // len(ORDER)
+            at = lax.rem(n, len(ORDER))
+            word = jnp.int32(ORDER[0])
+            for m in range(1, len(ORDER)):
+                word = jnp.where(at == m, jnp.int32(ORDER[m]), word)
+            for part in range(3):
+                code = word // 64**part
+                visit(lax.rem(code, 4), lax.rem(code // 4, 4), lax.rem(code // 16, 4), kc)
+            return carry
+
+        lax.fori_loop(0, len(ORDER), some, 0)
+        visit(0, 0, 0, 1)
+        lax.fori_loop(len(ORDER), 2 * len(ORDER), some, 0)
 
     def row_of(d, slot):
         return jnp.maximum(wanted[0, d * CAP + slot], 0)
@@ -178,22 +223,23 @@
         ref[2 * at] = table_u[row_of(d, 0)]
         ref[2 * at + 1] = table_u[row_of(d, 1)]
 
-    def send_part_a(k, carry):
-        di, dj = partner(k)
-        d = di * ny + dj
-        pack_a(send_a, d, d)
-        pltpu.make_async_remote_copy(
-            src_ref=send_a.at[pl.ds(2 * d, 2)],
-            dst_ref=recv_a.at[pl.ds(2 * me, 2)],
-            send_sem=send_sem.at[0],
-            recv_sem=recv_sem.at[0],
-            device_id=(di, dj),
-            device_id_type=MESH,
-        ).start()
-        return carry
-
-    lax.fori_loop(1, count, send_part_a, 0)
-    pack_a(recv_a, me, me)
+    def send(n, tiles, pack, out, landed):
+        def one(d, device):
+            pack(out, d, d)
+            pltpu.make_async_remote_copy(
+                src_ref=out.at[pl.ds(tiles * d, tiles)],
+                dst_ref=landed.at[pl.ds(tiles * me, tiles)],
+                send_sem=send_sem.at[n],
+                recv_sem=recv_sem.at[n],
+                device_id=device,
+                device_id_type=MESH,
+            ).start()
+
+        to_partners(one)
+        pack(landed, me, me)
+
+    small[0].wait()
+    send(0, 2, pack_a, send_a, recv_a)
 
     for copy in halo:
         copy.wait()
@@ -229,36 +275,32 @@
 
     loop(ROWS, 8, gradient_row)
 
-    def pack_b(ref, at, d):
+    def pack_c(ref, at, d):
         r0, r1 = row_of(d, 0), row_of(d, 1)
-        ref[3 * at] = table_g[r0]
-        ref[3 * at + 1] = table_g[r1]
         low = jnp.where(small_row < 4, table_lo[r0], pltpu.roll(table_lo[r1], 4, 0))
         high = jnp.where(small_lane < 64, table_hi[r0], pltpu.roll(table_hi[r1], 64, 1))
-        ref[3 * at + 2] = jnp.concatenate([low, high], 0).astype(BF16)
-
-    def send_part_b(k, carry):
-        di, dj = partner(k)
-        d = di * ny + dj
-        pack_b(send_b, d, d)
-        pltpu.make_async_remote_copy(
-            src_ref=send_b.at[pl.ds(3 * d, 3)],
-            dst_ref=recv_b.at[pl.ds(3 * me, 3)],
-            send_sem=send_sem.at[1],
-            recv_sem=recv_sem.at[1],
-            device_id=(di, dj),
-            device_id_type=MESH,
-        ).start()
-        return carry
-
-    lax.fori_loop(1, count, send_part_b, 0)
-    pack_b(recv_b, me, me)
-
+        ref[at] = jnp.concatenate([low, high], 0).astype(BF16)
+
+    send(1, 1, pack_c, send_c, recv_c)
+
+    def pack_b(ref, at, d):
+        ref[2 * at] = table_g[row_of(d, 0)]
+        ref[2 * at + 1] = table_g[row_of(d, 1)]
+
+    send(2, 2, pack_b, send_b, recv_b)
+
+    for copy in small[1:]:
+        copy.wait()
     get_weights.wait()
-    others = count - 1
-    for n, (out, landed, tiles) in enumerate(((send_a, recv_a, 2), (send_b, recv_b, 3))):
-        whole = pl.ds(0, tiles * others)
+    messages = ((send_a, recv_a, 2), (send_c, recv_c, 1), (send_b, recv_b, 2))
+
+    def landed_whole(n):
+        _, landed, tiles = messages[n]
+        whole = pl.ds(0, tiles * (count - 1))
         pltpu.make_async_copy(landed.at[whole], landed.at[whole], recv_sem.at[n]).wait()
+
+    landed_whole(0)
+    landed_whole(1)
 
     def grad_y(cells, west, east):
         lanes = iota(cells.shape, 1)
@@ -266,13 +308,16 @@
         inner = minmod(step, pltpu.roll(step, 1, 1))
         return jnp.where(lanes == 0, west, jnp.where(lanes == LANES - 1, east, inner))
 
-    def product(p):
+    is_volume = small_row == VOLUME - FULL
+    ones = jnp.ones((8, LANES), F32)
+    blank = jnp.zeros((8, LANES), F32)
+    none = jnp.zeros((FULL, LANES), BF16)
+
+    def first_terms(p):
         e = slots[0, p]
-        s = e // 2
         second = lax.rem(e, 2) == 1
         values = recv_a[e]
-        grads = recv_b[3 * s + lax.rem(e, 2)]
-        mixed = recv_b[3 * s + 2].astype(F32)
+        mixed = recv_c[e // 2].astype(F32)
         low, high = mixed[0:8], mixed[8:16]
         low = jnp.where(second, pltpu.roll(low, 4, 0), low)
         high = jnp.where(second, pltpu.roll(high, 64, 1), high)
@@ -281,21 +326,38 @@
         for n, cells in enumerate((wide[0:8], wide[8:16], low)):
             ends = pltpu.roll(high, LANES - 1 - 2 * n, 1)
             parts.append(grad_y(cells, ends, ends))
-        is_volume = small_row == VOLUME - FULL
-        blank = jnp.zeros((8, LANES), F32)
-        low_u = jnp.where(is_volume, jnp.ones((8, LANES), F32), low)
+        low_u = jnp.where(is_volume, ones, low)
         low_g = jnp.where(is_volume, blank, pltpu.roll(low, 6, 0))
         low_y = jnp.where(is_volume, blank, parts[2])
-        upper = jnp.concatenate(
-            [values, grads, jnp.concatenate(parts[:2], 0).astype(BF16)], 1
-        )
+        upper = jnp.concatenate([values, none, jnp.concatenate(parts[:2], 0).astype(BF16)], 1)
         lower = jnp.concatenate([low_u, low_g, low_y], 1).astype(BF16)
-        left = jnp.concatenate([upper, lower], 0)
-        contrib[pl.ds(pl.multiple_of(p * SLAB, SLAB), SLAB), :] = jnp.dot(
-            left, weights[p], preferred_element_type=F32
-        )
-
-    loop(PAIRS, 4, product)
+        return jnp.concatenate([upper, lower], 0)
+
+    def slab(p, size):
+        return pl.ds(pl.multiple_of(p * SLAB, SLAB), size)
+
+    def first_product(q):
+        p = 2 * q
+        left = jnp.concatenate([first_terms(p), first_terms(p + 1)], 0)
+        right = jnp.concatenate([weights[p], weights[p + 1]], 1)
+        both = jnp.dot(left, right, preferred_element_type=F32)
+        contrib[slab(p, SLAB), :] = both[:SLAB, :LANES]
+        contrib[slab(p + 1, SLAB), :] = both[SLAB:, LANES:]
+
+    loop(PAIRS // 2, 4, first_product)
+
+    landed_whole(2)
+
+    def second_product(q):
+        p = 2 * q
+        left = jnp.concatenate([recv_b[slots[0, p]], recv_b[slots[0, p + 1]]], 0)
+        middle = pl.ds(LANES, LANES)
+        right = jnp.concatenate([weights[p, middle, :], weights[p + 1, middle, :]], 1)
+        both = jnp.dot(left, right, preferred_element_type=F32)
+        contrib[slab(p, FULL), :] += both[:FULL, :LANES]
+        contrib[slab(p + 1, FULL), :] += both[FULL:, LANES:]
+
+    loop(PAIRS // 2, 14, second_product)
 
     chosen = (iota((ROWS, PAIRS), 0) == blocks[...]).astype(BF16)
 
@@ -315,7 +377,6 @@
         head = jnp.where(lane == f, pltpu.roll(cells, f, 1) if f else cells, head)
         tail = jnp.where(lane == f, pltpu.roll(cells, f + 1, 1), tail)
 
-    blank = jnp.zeros((8, LANES), F32)
     row_out2[0] = jnp.concatenate([u[pl.ds(ROWS - 1, SLAB, stride=ROWS), :], blank], 0).astype(BF16)
     row_out2[1] = jnp.concatenate([u[pl.ds(0, SLAB, stride=ROWS), :], blank], 0).astype(BF16)
     col_out2[0] = tail.astype(BF16)
@@ -342,12 +403,33 @@
     new_ref[...] = u[pl.ds(0, FIELDS * ROWS), :]
     for copy in halo:
         copy.wait()
-    norths = row_in2[0].astype(F32)
-    souths = row_in2[1].astype(F32)
-    wests = col_in2[0].astype(F32)
-    easts = col_in2[1].astype(F32)
+    row_ref[...] = row_in2[...]
+    col_ref[...] = col_in2[...]
+    for n, (out, _, tiles) in enumerate(messages):
+        whole = pl.ds(0, tiles * (count - 1))
+        pltpu.make_async_copy(out.at[whole], out.at[whole], send_sem.at[n]).wait()
+
+
+def finish(nx, ny, cells_ref, row_ref, col_ref, kappa_hbm, new_ref, flux_ref, flux, kappa, sem):
+    i = lax.axis_index("gx")
+    j = lax.axis_index("gy")
+    get_kappa = pltpu.make_async_copy(kappa_hbm, kappa, sem.at[0])
+    get_kappa.start()
+    put_new = pltpu.make_async_copy(cells_ref, new_ref, sem.at[1])
+    put_new.start()
+    first_x, last_x = i == 0, i == nx - 1
+    first_y, last_y = j == 0, j == ny - 1
+    lane = iota((ROWS, LANES), 1)
+    row = iota((ROWS, LANES), 0)
+    norths = row_ref[0].astype(F32)
+    souths = row_ref[1].astype(F32)
+    wests = col_ref[0].astype(F32)
+    easts = col_ref[1].astype(F32)
+    get_kappa.wait()
+    puts = []
     for f in range(FIELDS):
-        cells = field(u, f)
+        here = pl.ds(f * ROWS, ROWS)
+        cells = cells_ref[here, :]
         north = jnp.where(first_x, cells[0:1, :], norths[f : f + 1, :])
         south = jnp.where(last_x, cells[ROWS - 1 :, :], souths[f : f + 1, :])
         upper = jnp.where(row == 0, north, pltpu.roll(cells, 1, 0))
@@ -356,13 +438,14 @@
         east = jnp.where(last_y, cells, pltpu.roll(easts, LANES - 1 - f, 1))
         left = jnp.where(lane == 0, west, pltpu.roll(cells, 1, 1))
         right = jnp.where(lane == LANES - 1, east, pltpu.roll(cells, LANES - 1, 1))
-        flux_ref[pl.ds(f * ROWS, ROWS), :] = kappa[f] * (
-            upper + lower + left + right - 4.0 * cells
-        )
-
-    for n, (out, landed, tiles) in enumerate(((send_a, recv_a, 2), (send_b, recv_b, 3))):
-        whole = pl.ds(0, tiles * others)
-        pltpu.make_async_copy(out.at[whole], out.at[whole], send_sem.at[n]).wait()
+        flux[here, :] = kappa[f] * (upper + lower + left + right - 4.0 * cells)
+        if f % GROUP == GROUP - 1:
+            part = pl.ds((f + 1 - GROUP) * ROWS, GROUP * ROWS)
+            put = pltpu.make_async_copy(flux.at[part], flux_ref.at[part], sem.at[2 + f // GROUP])
+            put.start()
+            puts.append(put)
+    for put in [put_new] + puts:
+        put.wait()
 
 
 def shards(nx, ny, old_fields, send_block, pair_slot, pair_block, crossing, kappa):
@@ -370,14 +453,18 @@
     count = nx * ny
     flat = (FIELDS * ROWS, LANES)
     padded = (SLAB * ROWS, LANES)
-    any_space = pl.BlockSpec(memory_space=pl.ANY)
-    smem = pl.BlockSpec(memory_space=pltpu.SMEM)
+    hbm = pl.BlockSpec(memory_space=pltpu.HBM)
     vmem = pl.BlockSpec(memory_space=pltpu.VMEM)
-    new_fields, flux = pl.pallas_call(
+    in_hbm = lambda array: pltpu.with_memory_space_constraint(array, pltpu.HBM)
+    cells, edge_rows, edge_cols = pl.pallas_call(
         functools.partial(kernel, nx, ny),
-        out_shape=(jax.ShapeDtypeStruct(flat, F32), jax.ShapeDtypeStruct(flat, F32)),
-        in_specs=[any_space, any_space, smem, smem, vmem, smem],
-        out_specs=(vmem, vmem),
+        out_shape=(
+            jax.ShapeDtypeStruct(flat, F32),
+            jax.ShapeDtypeStruct((2, 32, LANES), BF16),
+            jax.ShapeDtypeStruct((2, ROWS, LANES), BF16),
+        ),
+        in_specs=[hbm] * 5,
+        out_specs=(vmem,) * 3,
         scratch_shapes=[
             pltpu.VMEM(padded, F32),
             pltpu.VMEM(flat, F32),
@@ -388,9 +475,14 @@
             pltpu.VMEM((ROWS, 8, LANES), F32),
             pltpu.VMEM((ROWS, 8, LANES), F32),
             pltpu.VMEM((2 * count, 16, LANES), BF16),
-            pltpu.VMEM((3 * count, 16, LANES), BF16),
             pltpu.VMEM((2 * count, 16, LANES), BF16),
-            pltpu.VMEM((3 * count, 16, LANES), BF16),
+            pltpu.VMEM((count, 16, LANES), BF16),
+            pltpu.VMEM((2 * count, 16, LANES), BF16),
+            pltpu.VMEM((2 * count, 16, LANES), BF16),
+            pltpu.VMEM((count, 16, LANES), BF16),
+            pltpu.SMEM((1, CAP * count), jnp.int32),
+            pltpu.SMEM((1, PAIRS), jnp.int32),
+            pltpu.VMEM((1, PAIRS), jnp.int32),
             pltpu.VMEM((PAIRS, 3 * LANES, LANES), BF16),
             pltpu.VMEM((PAIRS * SLAB, LANES), F32),
             pltpu.VMEM((2, SLAB, LANES), F32),
@@ -401,13 +493,13 @@
             pltpu.VMEM((2, 32, LANES), BF16),
             pltpu.VMEM((2, ROWS, LANES), BF16),
             pltpu.VMEM((2, ROWS, LANES), BF16),
-            pltpu.SemaphoreType.DMA((2,)),
+            pltpu.SemaphoreType.DMA((5,)),
             pltpu.SemaphoreType.DMA((4,)),
             pltpu.SemaphoreType.DMA((4,)),
             pltpu.SemaphoreType.DMA((4,)),
             pltpu.SemaphoreType.DMA((4,)),
-            pltpu.SemaphoreType.DMA((2,)),
-            pltpu.SemaphoreType.DMA((2,)),
+            pltpu.SemaphoreType.DMA((3,)),
+            pltpu.SemaphoreType.DMA((3,)),
         ],
         compiler_params=pltpu.CompilerParams(
             collective_id=0, has_side_effects=True, vmem_limit_bytes=48 * 2**20
@@ -418,13 +510,24 @@
             transcendentals=0,
         ),
     )(
-        old_fields.reshape(flat),
-        crossing.reshape(PAIRS, 3 * LANES, LANES),
-        send_block,
-        pair_slot,
-        pair_block,
-        kappa,
+        in_hbm(old_fields.reshape(flat)),
+        in_hbm(crossing.reshape(PAIRS, 3 * LANES, LANES)),
+        in_hbm(send_block),
+        in_hbm(pair_slot),
+        in_hbm(pair_block),
     )
+    new_fields, flux = pl.pallas_call(
+        functools.partial(finish, nx, ny),
+        out_shape=(jax.ShapeDtypeStruct(flat, F32), jax.ShapeDtypeStruct(flat, F32)),
+        in_specs=[vmem] * 3 + [hbm],
+        out_specs=(hbm, hbm),
+        scratch_shapes=[
+            pltpu.VMEM(flat, F32),
+            pltpu.SMEM((FIELDS,), F32),
+            pltpu.SemaphoreType.DMA((2 + FIELDS // GROUP,)),
+        ],
+        compiler_params=pltpu.CompilerParams(vmem_limit_bytes=4 * 2**20),
+    )(cells, edge_rows, edge_cols, in_hbm(kappa))
     return new_fields.reshape(shape), flux.reshape(shape)
 
 

time: 65.1 us -> 51.6 us (0.79)
  Pallas kernels: 58.9 us -> 50.8 us
  local copies, waits for them, and re-layouts: 5.33 us -> 0 us
    pallas_call x1, Pallas kernels: 58.9 us -> 48.9 us  [shards(): pl.pallas_call(functools.partial(kernel, nx, ny), out_shape=(jax.ShapeDty...]
    unnamed x12 -> x0, local copies, waits for them, and re-layouts: 5.33 us -> none
    pallas_call x0 -> x1, Pallas kernels: none -> 1.91 us  [shards(): pl.pallas_call(functools.partial(finish, nx, ny), out_shape=(jax.ShapeDty...]
where the time goes in v2:
time: 51.6 us; the launch traced here: 51.5 us
  Pallas kernels  50.8 us (98%)
  between operations  0.64 us (1%)
    pallas_call x1, Pallas kernels, shards(): pl.pallas_call(functools.partial(kernel, nx, ny), out_shape=(jax.ShapeDty...  48.9 us
    pallas_call x1, Pallas kernels, shards(): pl.pallas_call(functools.partial(finish, nx, ny), out_shape=(jax.ShapeDty...  1.91 us

profile of v2, /device:TPU:1, one launch (start us, length us, event | category | flops | bytes accessed | tf_op | source)
XLA Modules:
  0.0 51.5 jit_solution(12042073675094508531)
XLA Ops:
  0.6 48.9 %shard_map.77 = (f32[1152,128]{1,0:T(8,128)S(1)}, bf16[2,32,128]{2,1,0:T(8,128)(2,1)S(1)}, bf16[2,64,128]{2,1,0:T(8,128)(2,1)S(1)}) custom-call(f32[1152,128]{1,0:T(8,128)} %bitcast.5, bf16[112,384,128]{2,1,0:T(8,128)(2,1)} %bitcast.4, s32[1,256]{1,0:T(1,128)} %wanted_hbm.1, s32[1,112]{1,0:T(1,128)} %slots_hbm.1, s32[1,112]{1,0:T(1,128)} %blocks_hbm.1), custom_call_target="tpu_custom_call" | custom-call | flops 264241152 | bytes 12582912 | tf_op jit(solution)/shard_map/pallas_call | solution.py:459
  49.6 1.9 %shard_map.78 = (f32[1152,128]{1,0:T(8,128)}, f32[1152,128]{1,0:T(8,128)}) custom-call(f32[1152,128]{1,0:T(8,128)S(1)} %get-tuple-element.7.cells_ref, bf16[2,32,128]{2,1,0:T(8,128)(2,1)S(1)} %get-tuple-element.8.row_ref, bf16[2,64,128]{2,1,0:T(8,128)(2,1)S(1)} %get-tuple-element.9.col_ref, f32[18]{0:T(128)} %kappa_hbm.1), custom_call_target="tpu_custom_call" | custom-call | tf_op jit(solution)/shard_map/pallas_call | solution.py:519

commit v3 on v2

v3 whole, which is shorter than its diff:
```python
import functools

import jax
import jax.numpy as jnp
from jax import lax
from jax.experimental import pallas as pl
from jax.experimental.pallas import tpu as pltpu
from jax.sharding import PartitionSpec as P

MESH = pl.DeviceIdType.MESH
F32 = jnp.float32
BF16 = jnp.bfloat16

FIELDS = 18
FULL = 16
ROWS = 64
LANES = 128
PAIRS = 112
CAP = 2
SLAB = 24
VOLUME = 18


def chip_offsets():
    groups, seen = [], {(0, 0, 0)}
    for code in range(1, 64):
        offset = (code // 16, code // 4 % 4, code % 4)
        group = []
        for sign in (1, -1):
            for turn in range(3):
                other = tuple(sign * offset[(turn + axis) % 3] % 4 for axis in range(3))
                if other not in seen:
                    seen.add(other)
                    group.append(other)
        if group:
            groups.append(group)
    groups.sort(key=lambda group: -sum(min(step, 4 - step) for step in group[0]))
    codes = [kx + 4 * ky + 16 * kz for group in groups for kx, ky, kz in group]
    return [sum(codes[n + m] * 64**m for m in range(3)) for n in range(0, len(codes), 3)]


ORDER = chip_offsets()


def minmod(first, second):
    least = jnp.where(first > 0.0, jnp.minimum(first, second), jnp.maximum(first, second))
    return jnp.where(first * second > 0.0, least, jnp.zeros_like(first))


def iota(shape, axis):
    return lax.broadcasted_iota(jnp.int32, shape, axis)


def loop(count, step, body):
    def outer(n, carry):
        for part in range(step):
            body(n * step + part)
        return carry

    lax.fori_loop(0, count // step, outer, 0)


def kernel(
    nx,
    ny,
    old_hbm,
    crossing_hbm,
    wanted_hbm,
    slots_hbm,
    blocks_hbm,
    kappa_hbm,
    new_ref,
    flux_ref,
    u,
    gx,
    inner,
    rest,
    table_u,
    table_g,
    table_lo,
    table_e,
    send_a,
    send_b,
    send_c,
    send_e,
    recv_a,
    recv_b,
    recv_c,
    recv_e,
    edges_in,
    edge_tiles,
    wanted,
    slots,
    blocks,
    kappa,
    weights,
    contrib,
    volume,
    row_out,
    row_in,
    col_out,
    col_in,
    row_out2,
    row_in2,
    col_out2,
    col_in2,
    local_sem,
    halo_send,
    halo_recv,
    halo_send2,
    halo_recv2,
    send_sem,
    recv_sem,
):
    i = lax.axis_index("gx")
    j = lax.axis_index("gy")
    count = nx * ny
    me = i * ny + j

    get_old = pltpu.make_async_copy(old_hbm, u.at[pl.ds(0, FIELDS * ROWS)], local_sem.at[0])
    get_old.start()
    small = []
    for n, (source, target) in enumerate(
        ((wanted_hbm, wanted), (slots_hbm, slots), (blocks_hbm, blocks), (kappa_hbm, kappa))
    ):
        copy = pltpu.make_async_copy(source, target, local_sem.at[2 + n])
        copy.start()
        small.append(copy)
    get_weights = pltpu.make_async_copy(crossing_hbm, weights, local_sem.at[1])
    get_weights.start()

    barrier = pltpu.get_barrier_semaphore()

    def greet(k, carry):
        for core in range(2):
            di = lax.rem(i // 4 + 2 + k // 4, 4) * 4 + lax.rem(i + 2 + k, 4)
            dj = lax.rem(lax.rem(j, 2) + core, 2)
            for step in range(4):
                signal(di, lax.rem(j // 2 + 2 + step, 4) * 2 + dj)
        return carry

    def signal(di, dj):
        @pl.when(di * ny + dj != me)
        def _():
            pl.semaphore_signal(barrier, inc=1, device_id=(di, dj), device_id_type=MESH)

    lax.fori_loop(0, nx, greet, 0)

    after_x = (lax.rem(i + 1, nx), j)
    before_x = (lax.rem(i + nx - 1, nx), j)
    after_y = (i, lax.rem(j + 1, ny))
    before_y = (i, lax.rem(j + ny - 1, ny))
    first_x, last_x = i == 0, i == nx - 1
    first_y, last_y = j == 0, j == ny - 1

    lane = iota((ROWS, LANES), 1)
    row = iota((ROWS, LANES), 0)

    def field(ref, f):
        return ref[pl.ds(f * ROWS, ROWS), :]

    zeros = jnp.zeros((ROWS, LANES), F32)
    for f in range(FIELDS, SLAB):
        u[pl.ds(f * ROWS, ROWS), :] = zeros
    for f in range(4, 8):
        rest[pl.ds(f * ROWS, ROWS), :] = zeros
    get_old.wait()
    row_out[0] = u[pl.ds(ROWS - 1, SLAB, stride=ROWS), :]
    row_out[1] = u[pl.ds(0, SLAB, stride=ROWS), :]
    columns = [zeros] * 4
    for f in range(FIELDS):
        cells = field(u, f)
        for n, back in enumerate((0, 1, LANES - 2, LANES - 1)):
            shift = (f - back) % LANES
            moved = pltpu.roll(cells, shift, 1) if shift else cells
            columns[n] = jnp.where(lane == f, moved, columns[n])
    col_out[0] = columns[3]
    col_out[1] = columns[0]
    inner[0] = columns[1]
    inner[1] = columns[2]

    def value_row(r):
        table_u[r] = u[pl.ds(r, FULL, stride=ROWS), :].astype(BF16)

    loop(ROWS, 8, value_row)

    pl.semaphore_wait(barrier, count - 1)

    def exchange(sources, targets, sends, receives):
        copies = []
        for n, device in enumerate((after_x, before_x, after_y, before_y)):
            copy = pltpu.make_async_remote_copy(
                src_ref=sources[n],
                dst_ref=targets[n],
                send_sem=sends.at[n],
                recv_sem=receives.at[n],
                device_id=device,
                device_id_type=MESH,
            )
            pl.when(jnp.logical_not((last_x, first_x, last_y, first_y)[n]))(copy.start)
            copies.append(copy)
        return copies

    def exchanged(copies):
        for n, copy in enumerate(copies):
            pl.when(jnp.logical_not((last_x, first_x, last_y, first_y)[n]))(copy.wait_send)
            pl.when(jnp.logical_not((first_x, last_x, first_y, last_y)[n]))(copy.wait_recv)

    halo = exchange(
        (row_out.at[0], row_out.at[1], col_out.at[0], col_out.at[1]),
        (row_in.at[0], row_in.at[1], col_in.at[0], col_in.at[1]),
        halo_send,
        halo_recv,
    )

    y, z = i // 4, lax.rem(i, 4)
    x, c = j // 2, lax.rem(j, 2)

    def to_partners(body):
        def visit(kx, ky, kz, kc):
            di = lax.rem(y + ky, 4) * 4 + lax.rem(z + kz, 4)
            dj = lax.rem(x + kx, 4) * 2 + lax.rem(c + kc, 2)
            body(di * ny + dj, (di, dj))

        def some(n, carry):
            kc = n // len(ORDER)
            at = lax.rem(n, len(ORDER))
            word = jnp.int32(ORDER[0])
            for m in range(1, len(ORDER)):
                word = jnp.where(at == m, jnp.int32(ORDER[m]), word)
            for part in range(3):
                code = word // 64**part
                visit(lax.rem(code, 4), lax.rem(code // 4, 4), lax.rem(code // 16, 4), kc)
            return carry

        lax.fori_loop(0, len(ORDER), some, 0)
        visit(0, 0, 0, 1)
        lax.fori_loop(len(ORDER), 2 * len(ORDER), some, 0)

    def row_of(d, slot):
        return jnp.maximum(wanted[0, d * CAP + slot], 0)

    def pack_a(ref, at, d):
        ref[2 * at] = table_u[row_of(d, 0)]
        ref[2 * at + 1] = table_u[row_of(d, 1)]

    def send(*parts):
        def one(d, device):
            for n, tiles, pack, out, landed in parts:
                pack(out, d, d)
                pltpu.make_async_remote_copy(
                    src_ref=out.at[pl.ds(tiles * d, tiles)],
                    dst_ref=landed.at[pl.ds(tiles * me, tiles)],
                    send_sem=send_sem.at[n],
                    recv_sem=recv_sem.at[n],
                    device_id=device,
                    device_id_type=MESH,
                ).start()

        to_partners(one)
        for n, tiles, pack, out, landed in parts:
            pack(landed, me, me)

    small[0].wait()
    send((0, 2, pack_a, send_a, recv_a))

    exchanged(halo)
    for f in range(FIELDS):
        cells = field(u, f)
        north = jnp.where(first_x, cells[0:1, :], row_in[0, f : f + 1, :])
        south = jnp.where(last_x, cells[ROWS - 1 :, :], row_in[1, f : f + 1, :])
        upper = jnp.where(row == 0, north, pltpu.roll(cells, 1, 0))
        lower = jnp.where(row == ROWS - 1, south, pltpu.roll(cells, ROWS - 1, 0))
        grad = minmod(lower - cells, cells - upper)
        gx[pl.ds(f * ROWS, ROWS), :] = grad
        if f >= FULL:
            rest[pl.ds((f - FULL) * ROWS, ROWS), :] = cells
            rest[pl.ds((2 + f - FULL) * ROWS, ROWS), :] = grad

    head, tail = col_out[1], col_out[0]
    west = jnp.where(first_y, head, col_in[0])
    east = jnp.where(last_y, tail, col_in[1])
    edges = minmod(inner[0] - head, head - west)
    edges = jnp.where(
        lane < SLAB, edges, pltpu.roll(minmod(east - tail, tail - inner[1]), SLAB, 1)
    )
    edges = jnp.where(lane < 2 * SLAB, edges, 0.0)
    table_e[0] = edges
    table_e[1] = pltpu.roll(edges, 64, 1)

    small_lane = iota((8, LANES), 1)
    small_row = iota((8, LANES), 0)

    def gradient_row(r):
        table_g[r] = gx[pl.ds(r, FULL, stride=ROWS), :].astype(BF16)
        table_lo[r] = rest[pl.ds(r, 8, stride=ROWS), :]

    loop(ROWS, 8, gradient_row)

    def pack_c(ref, at, d):
        low = jnp.where(
            small_row < 4, table_lo[row_of(d, 0)], pltpu.roll(table_lo[row_of(d, 1)], 4, 0)
        )
        ref[at] = low.astype(BF16)

    def pack_e(ref, at, d):
        ref[at] = table_e[0, pl.ds(row_of(d, 0), 1), :] + table_e[1, pl.ds(row_of(d, 1), 1), :]

    send((1, 1, pack_c, send_c, recv_c), (3, 1, pack_e, send_e, recv_e))

    def pack_b(ref, at, d):
        ref[2 * at] = table_g[row_of(d, 0)]
        ref[2 * at + 1] = table_g[row_of(d, 1)]

    send((2, 2, pack_b, send_b, recv_b))

    for copy in small[1:]:
        copy.wait()
    get_weights.wait()
    messages = (
        (send_a, recv_a, 2),
        (send_c, recv_c, 1),
        (send_b, recv_b, 2),
        (send_e, recv_e, 1),
    )

    def landed_whole(n):
        _, landed, tiles = messages[n]
        whole = pl.ds(0, tiles * (count - 1))
        pltpu.make_async_copy(landed.at[whole], landed.at[whole], recv_sem.at[n]).wait()

    landed_whole(0)
    landed_whole(1)
    landed_whole(3)

    def edge_row(source):
        edges_in[pl.ds(source, 1), :] = recv_e[source]

    loop(count, 8, edge_row)
    turned = edges_in[...].T
    even = lax.rem(iota((SLAB, LANES), 1), 2) == 0
    for slot in range(CAP):
        west = turned[64 * slot : 64 * slot + SLAB]
        east = pltpu.roll(turned[64 * slot + SLAB : 64 * slot + 2 * SLAB], LANES - 1, 1)
        edges_in[pl.ds(slot * SLAB, SLAB), :] = jnp.where(even, west, east)
        edges_in[pl.ds((CAP + slot) * SLAB, SLAB), :] = jnp.where(even, east, west)

    def edge_tile(half):
        for odd in range(2):
            source = 2 * half + odd
            for slot in range(CAP):
                at = edges_in[pl.ds((CAP * odd + slot) * SLAB, SLAB), :]
                edge_tiles[CAP * source + slot] = pltpu.roll(at, LANES - source, 1)

    loop(count // 2, 4, edge_tile)

    def grad_y(cells, ends):
        lanes = iota(cells.shape, 1)
        step = pltpu.roll(cells, LANES - 1, 1) - cells
        inner = minmod(step, pltpu.roll(step, 1, 1))
        return jnp.where(jnp.logical_or(lanes == 0, lanes == LANES - 1), ends, inner)

    is_volume = small_row == VOLUME - FULL
    ones = jnp.ones((8, LANES), F32)
    blank = jnp.zeros((8, LANES), F32)
    none = jnp.zeros((FULL, LANES), BF16)

    def first_terms(p):
        e = slots[0, p]
        second = lax.rem(e, 2) == 1
        values = recv_a[e]
        low = recv_c[e // 2].astype(F32)
        low = jnp.where(second, pltpu.roll(low, 4, 0), low)
        wide = values.astype(F32)
        ends = edge_tiles[e]
        parts = [
            grad_y(cells, ends[8 * n : 8 * n + 8])
            for n, cells in enumerate((wide[0:8], wide[8:16], low))
        ]
        low_u = jnp.where(is_volume, ones, low)
        low_g = jnp.where(is_volume, blank, pltpu.roll(low, 6, 0))
        low_y = jnp.where(is_volume, blank, parts[2])
        upper = jnp.concatenate([values, none, jnp.concatenate(parts[:2], 0).astype(BF16)], 1)
        lower = jnp.concatenate([low_u, low_g, low_y], 1).astype(BF16)
        return jnp.concatenate([upper, lower], 0)

    def slab(p, size):
        return pl.ds(pl.multiple_of(p * SLAB, SLAB), size)

    def first_product(q):
        p = 2 * q
        left = jnp.concatenate([first_terms(p), first_terms(p + 1)], 0)
        right = jnp.concatenate([weights[p], weights[p + 1]], 1)
        both = jnp.dot(left, right, preferred_element_type=F32)
        contrib[slab(p, SLAB), :] = both[:SLAB, :LANES]
        contrib[slab(p + 1, SLAB), :] = both[SLAB:, LANES:]

    loop(PAIRS // 2, 7, first_product)

    chosen = (iota((ROWS, PAIRS), 0) == blocks[...]).astype(BF16)

    def gathered(f):
        terms = contrib[pl.ds(f, PAIRS, stride=SLAB), :]
        high = terms.astype(BF16)
        low = (terms - high.astype(F32)).astype(BF16)
        return jnp.dot(chosen, high, preferred_element_type=F32) + jnp.dot(
            chosen, low, preferred_element_type=F32
        )

    volume[...] = gathered(VOLUME)
    for f in range(FIELDS):
        u[pl.ds(f * ROWS, ROWS), :] = gathered(f)

    landed_whole(2)

    def second_product(q):
        p = 2 * q
        left = jnp.concatenate([recv_b[slots[0, p]], recv_b[slots[0, p + 1]]], 0)
        middle = pl.ds(LANES, LANES)
        right = jnp.concatenate([weights[p, middle, :], weights[p + 1, middle, :]], 1)
        both = jnp.dot(left, right, preferred_element_type=F32)
        contrib[slab(p, FULL), :] = both[:FULL, :LANES]
        contrib[slab(p + 1, FULL), :] = both[FULL:, LANES:]

    loop(PAIRS // 2, 14, second_product)

    head, tail = zeros, zeros
    for f in range(FIELDS):
        cells = field(u, f)
        if f < FULL:
            cells = cells + gathered(f)
        cells = cells / volume[...]
        u[pl.ds(f * ROWS, ROWS), :] = cells
        head = jnp.where(lane == 2 * f, pltpu.roll(cells, 2 * f, 1) if f else cells, head)
        tail = jnp.where(lane == 2 * f + 1, pltpu.roll(cells, 2 * f + 2, 1), tail)

    row_out2[0] = jnp.concatenate([u[pl.ds(ROWS - 1, SLAB, stride=ROWS), :], blank], 0).astype(BF16)
    row_out2[1] = jnp.concatenate([u[pl.ds(0, SLAB, stride=ROWS), :], blank], 0).astype(BF16)
    col_out2[0] = tail.astype(BF16)
    col_out2[1] = head.astype(BF16)
    halo = exchange(
        (row_out2.at[0], row_out2.at[1], col_out2.at[0], col_out2.at[1]),
        (row_in2.at[0], row_in2.at[1], col_in2.at[0], col_in2.at[1]),
        halo_send2,
        halo_recv2,
    )
    ends = jnp.logical_or(lane == 0, lane == LANES - 1)
    for f in range(FIELDS):
        here = pl.ds(f * ROWS, ROWS)
        cells = field(u, f)
        new_ref[here, :] = cells
        upper = jnp.where(row == 0, jnp.where(first_x, cells, 0.0), pltpu.roll(cells, 1, 0))
        lower = jnp.where(
            row == ROWS - 1, jnp.where(last_x, cells, 0.0), pltpu.roll(cells, ROWS - 1, 0)
        )
        left = jnp.where(lane == 0, jnp.where(first_y, cells, 0.0), pltpu.roll(cells, 1, 1))
        right = jnp.where(
            lane == LANES - 1, jnp.where(last_y, cells, 0.0), pltpu.roll(cells, LANES - 1, 1)
        )
        flux_ref[here, :] = kappa[f] * (upper + lower + left + right - 4.0 * cells)
    exchanged(halo)
    norths = jnp.where(first_x, 0.0, row_in2[0].astype(F32))
    souths = jnp.where(last_x, 0.0, row_in2[1].astype(F32))
    sides = jnp.where(first_y, 0.0, col_in2[0].astype(F32)) + jnp.where(
        last_y, 0.0, col_in2[1].astype(F32)
    )
    for f in range(FIELDS):
        here = pl.ds(f * ROWS, ROWS)
        outer = jnp.where(ends, pltpu.roll(sides, LANES - 1 - 2 * f, 1), 0.0)
        outer = outer + jnp.where(row == 0, norths[f : f + 1, :], 0.0)
        outer = outer + jnp.where(row == ROWS - 1, souths[f : f + 1, :], 0.0)
        flux_ref[here, :] += kappa[f] * outer

    for n, (out, _, tiles) in enumerate(messages):
        whole = pl.ds(0, tiles * (count - 1))
        pltpu.make_async_copy(out.at[whole], out.at[whole], send_sem.at[n]).wait()


def finish(cells, flux, cells_out, flux_out, sem):
    copies = [
        pltpu.make_async_copy(cells, cells_out, sem.at[0]),
        pltpu.make_async_copy(flux, flux_out, sem.at[1]),
    ]
    for copy in copies:
        copy.start()
    for copy in copies:
        copy.wait()


def shards(nx, ny, old_fields, send_block, pair_slot, pair_block, crossing, kappa):
    shape = old_fields.shape
    count = nx * ny
    flat = (FIELDS * ROWS, LANES)
    padded = (SLAB * ROWS, LANES)
    hbm = pl.BlockSpec(memory_space=pltpu.HBM)
    vmem = pl.BlockSpec(memory_space=pltpu.VMEM)
    in_hbm = lambda array: pltpu.with_memory_space_constraint(array, pltpu.HBM)
    cells, fluxes = pl.pallas_call(
        functools.partial(kernel, nx, ny),
        out_shape=(
            jax.ShapeDtypeStruct(flat, F32),
            jax.ShapeDtypeStruct(flat, F32),
        ),
        in_specs=[hbm] * 6,
        out_specs=(vmem, vmem),
        scratch_shapes=[
            pltpu.VMEM(padded, F32),
            pltpu.VMEM(flat, F32),
            pltpu.VMEM((2, ROWS, LANES), F32),
            pltpu.VMEM((8 * ROWS, LANES), F32),
            pltpu.VMEM((ROWS, FULL, LANES), BF16),
            pltpu.VMEM((ROWS, FULL, LANES), BF16),
            pltpu.VMEM((ROWS, 8, LANES), F32),
            pltpu.VMEM((2, ROWS, LANES), F32),
            pltpu.VMEM((2 * count, 16, LANES), BF16),
            pltpu.VMEM((2 * count, 16, LANES), BF16),
            pltpu.VMEM((count, 8, LANES), BF16),
            pltpu.VMEM((count, 1, LANES), F32),
            pltpu.VMEM((2 * count, 16, LANES), BF16),
            pltpu.VMEM((2 * count, 16, LANES), BF16),
            pltpu.VMEM((count, 8, LANES), BF16),
            pltpu.VMEM((count, 1, LANES), F32),
            pltpu.VMEM((count, LANES), F32),
            pltpu.VMEM((CAP * count, SLAB, LANES), F32),
            pltpu.SMEM((1, CAP * count), jnp.int32),
            pltpu.SMEM((1, PAIRS), jnp.int32),
            pltpu.VMEM((1, PAIRS), jnp.int32),
            pltpu.SMEM((FIELDS,), F32),
            pltpu.VMEM((PAIRS, 3 * LANES, LANES), BF16),
            pltpu.VMEM((PAIRS * SLAB, LANES), F32),
            pltpu.VMEM((ROWS, LANES), F32),
            pltpu.VMEM((2, SLAB, LANES), F32),
            pltpu.VMEM((2, SLAB, LANES), F32),
            pltpu.VMEM((2, ROWS, LANES), F32),
            pltpu.VMEM((2, ROWS, LANES), F32),
            pltpu.VMEM((2, 32, LANES), BF16),
            pltpu.VMEM((2, 32, LANES), BF16),
            pltpu.VMEM((2, ROWS, LANES), BF16),
            pltpu.VMEM((2, ROWS, LANES), BF16),
            pltpu.SemaphoreType.DMA((6,)),
            pltpu.SemaphoreType.DMA((4,)),
            pltpu.SemaphoreType.DMA((4,)),
            pltpu.SemaphoreType.DMA((4,)),
            pltpu.SemaphoreType.DMA((4,)),
            pltpu.SemaphoreType.DMA((4,)),
            pltpu.SemaphoreType.DMA((4,)),
        ],
        compiler_params=pltpu.CompilerParams(
            collective_id=0, has_side_effects=True, vmem_limit_bytes=48 * 2**20
        ),
        cost_estimate=pl.CostEstimate(
            flops=2 * PAIRS * 3 * LANES * LANES * SLAB,
            bytes_accessed=12 * 2**20,
            transcendentals=0,
        ),
    )(
        in_hbm(old_fields.reshape(flat)),
        in_hbm(crossing.reshape(PAIRS, 3 * LANES, LANES)),
        in_hbm(send_block),
        in_hbm(pair_slot),
        in_hbm(pair_block),
        in_hbm(kappa),
    )
    new_fields, flux = pl.pallas_call(
        finish,
        out_shape=(jax.ShapeDtypeStruct(flat, F32), jax.ShapeDtypeStruct(flat, F32)),
        in_specs=[vmem, vmem],
        out_specs=(hbm, hbm),
        scratch_shapes=[pltpu.SemaphoreType.DMA((2,))],
        compiler_params=pltpu.CompilerParams(vmem_limit_bytes=4 * 2**20),
    )(cells, fluxes)
    return new_fields.reshape(shape), flux.reshape(shape)


def solution(mesh):
    placed = (
        P(None, "gx", "gy"),
        P(("gx", "gy"), None),
        P(("gx", "gy"), None),
        P(("gx", "gy"), None),
        P(("gx", "gy"), None, None, None, None),
        P(),
    )
    return jax.shard_map(
        functools.partial(shards, mesh.shape["gx"], mesh.shape["gy"]),
        mesh=mesh,
        in_specs=placed,
        out_specs=(P(None, "gx", "gy"), P(None, "gx", "gy")),
        check_vma=False,
    )
```

time: 51.6 us -> 46.8 us (0.907)
  Pallas kernels: 50.8 us -> 45.9 us
    pallas_call x1, Pallas kernels: 48.9 us -> 44.9 us  [shards(): pl.pallas_call(functools.partial(kernel, nx, ny), out_shape=(jax.ShapeDty...]
    pallas_call x1, Pallas kernels: 1.91 us -> 1.03 us  [shards(): pl.pallas_call(finish, out_shape=(jax.ShapeDtypeStruct(flat, F32), jax.Sh...]
where the time goes in v3:
time: 46.8 us; the launch traced here: 46.5 us
  Pallas kernels  45.9 us (98%)
  between operations  0.64 us (1%)
    pallas_call x1, Pallas kernels, shards(): pl.pallas_call(functools.partial(kernel, nx, ny), out_shape=(jax.ShapeDty...  44.9 us
    pallas_call x1, Pallas kernels, shards(): pl.pallas_call(finish, out_shape=(jax.ShapeDtypeStruct(flat, F32), jax.Sh...  1.03 us

profile of v3, /device:TPU:1, one launch (start us, length us, event | category | flops | bytes accessed | tf_op | source)
XLA Modules:
  0.0 46.5 jit_solution(2053287476409349495)
XLA Ops:
  0.6 44.9 %shard_map.77 = (f32[1152,128]{1,0:T(8,128)S(1)}, f32[1152,128]{1,0:T(8,128)S(1)}) custom-call(f32[1152,128]{1,0:T(8,128)} %bitcast.5, bf16[112,384,128]{2,1,0:T(8,128)(2,1)} %bitcast.4, s32[1,256]{1,0:T(1,128)} %wanted_hbm.1, s32[1,112]{1,0:T(1,128)} %slots_hbm.1, s32[1,112]{1,0:T(1,128)} %blocks_hbm.1, f32[18]{0:T(128)} %kappa_hbm.1), custom_call_target="tpu_custom_call" | custom-call | flops 264241152 | bytes 12582912 | tf_op jit(solution)/shard_map/pallas_call | solution.py:498
  45.5 1.0 %shard_map.78 = (f32[1152,128]{1,0:T(8,128)}, f32[1152,128]{1,0:T(8,128)}) custom-call(f32[1152,128]{1,0:T(8,128)S(1)} %get-tuple-element.6.cells, f32[1152,128]{1,0:T(8,128)S(1)} %get-tuple-element.7.flux), custom_call_target="tpu_custom_call" | custom-call | tf_op jit(solution)/shard_map/pallas_call | solution.py:564

commit v4 on v3

--- a/solution.py
+++ b/solution.py
@@ -87,8 +87,8 @@
     recv_b,
     recv_c,
     recv_e,
-    edges_in,
-    edge_tiles,
+    end_rows,
+    pair_rows,
     wanted,
     slots,
     blocks,
@@ -197,9 +197,12 @@
                 device_id=device,
                 device_id_type=MESH,
             )
-            pl.when(jnp.logical_not((last_x, first_x, last_y, first_y)[n]))(copy.start)
             copies.append(copy)
         return copies
+
+    def start_exchange(copies, which):
+        for n in which:
+            pl.when(jnp.logical_not((last_x, first_x, last_y, first_y)[n]))(copies[n].start)
 
     def exchanged(copies):
         for n, copy in enumerate(copies):
@@ -212,30 +215,33 @@
         halo_send,
         halo_recv,
     )
+    start_exchange(halo, range(4))
 
     y, z = i // 4, lax.rem(i, 4)
     x, c = j // 2, lax.rem(j, 2)
 
-    def to_partners(body):
+    def to_partners(body, together):
         def visit(kx, ky, kz, kc):
             di = lax.rem(y + ky, 4) * 4 + lax.rem(z + kz, 4)
             dj = lax.rem(x + kx, 4) * 2 + lax.rem(c + kc, 2)
             body(di * ny + dj, (di, dj))
 
         def some(n, carry):
-            kc = n // len(ORDER)
             at = lax.rem(n, len(ORDER))
             word = jnp.int32(ORDER[0])
             for m in range(1, len(ORDER)):
                 word = jnp.where(at == m, jnp.int32(ORDER[m]), word)
             for part in range(3):
                 code = word // 64**part
-                visit(lax.rem(code, 4), lax.rem(code // 4, 4), lax.rem(code // 16, 4), kc)
+                kx, ky, kz = lax.rem(code, 4), lax.rem(code // 4, 4), lax.rem(code // 16, 4)
+                for kc in (0, 1) if together else (n // len(ORDER),):
+                    visit(kx, ky, kz, kc)
             return carry
 
         lax.fori_loop(0, len(ORDER), some, 0)
         visit(0, 0, 0, 1)
-        lax.fori_loop(len(ORDER), 2 * len(ORDER), some, 0)
+        if not together:
+            lax.fori_loop(len(ORDER), 2 * len(ORDER), some, 0)
 
     def row_of(d, slot):
         return jnp.maximum(wanted[0, d * CAP + slot], 0)
@@ -244,7 +250,7 @@
         ref[2 * at] = table_u[row_of(d, 0)]
         ref[2 * at + 1] = table_u[row_of(d, 1)]
 
-    def send(*parts):
+    def send(*parts, together=True):
         def one(d, device):
             for n, tiles, pack, out, landed in parts:
                 pack(out, d, d)
@@ -257,12 +263,12 @@
                     device_id_type=MESH,
                 ).start()
 
-        to_partners(one)
+        to_partners(one, together)
         for n, tiles, pack, out, landed in parts:
             pack(landed, me, me)
 
     small[0].wait()
-    send((0, 2, pack_a, send_a, recv_a))
+    send((0, 2, pack_a, send_a, recv_a), together=False)
 
     exchanged(halo)
     for f in range(FIELDS):
@@ -329,75 +335,86 @@
         whole = pl.ds(0, tiles * (count - 1))
         pltpu.make_async_copy(landed.at[whole], landed.at[whole], recv_sem.at[n]).wait()
 
-    landed_whole(0)
-    landed_whole(1)
-    landed_whole(3)
-
-    def edge_row(source):
-        edges_in[pl.ds(source, 1), :] = recv_e[source]
-
-    loop(count, 8, edge_row)
-    turned = edges_in[...].T
-    even = lax.rem(iota((SLAB, LANES), 1), 2) == 0
-    for slot in range(CAP):
-        west = turned[64 * slot : 64 * slot + SLAB]
-        east = pltpu.roll(turned[64 * slot + SLAB : 64 * slot + 2 * SLAB], LANES - 1, 1)
-        edges_in[pl.ds(slot * SLAB, SLAB), :] = jnp.where(even, west, east)
-        edges_in[pl.ds((CAP + slot) * SLAB, SLAB), :] = jnp.where(even, east, west)
-
-    def edge_tile(half):
-        for odd in range(2):
-            source = 2 * half + odd
-            for slot in range(CAP):
-                at = edges_in[pl.ds((CAP * odd + slot) * SLAB, SLAB), :]
-                edge_tiles[CAP * source + slot] = pltpu.roll(at, LANES - source, 1)
-
-    loop(count // 2, 4, edge_tile)
-
-    def grad_y(cells, ends):
+    def grad_y(cells):
         lanes = iota(cells.shape, 1)
         step = pltpu.roll(cells, LANES - 1, 1) - cells
-        inner = minmod(step, pltpu.roll(step, 1, 1))
-        return jnp.where(jnp.logical_or(lanes == 0, lanes == LANES - 1), ends, inner)
+        inside = jnp.logical_and(lanes > 0, lanes < LANES - 1)
+        return jnp.where(inside, minmod(step, pltpu.roll(step, 1, 1)), 0.0)
+
+    def slab(p, size, start=0):
+        return pl.ds(pl.multiple_of(p * SLAB + start, 8), size)
+
+    def weight(p, k):
+        return weights[p, pl.ds(k * LANES, LANES), :]
+
+    def upper_terms(p):
+        values = recv_a[slots[0, p]]
+        return jnp.concatenate([values, grad_y(values.astype(F32)).astype(BF16)], 1)
+
+    def upper_product(q):
+        p = 2 * q
+        left = jnp.concatenate([upper_terms(p), upper_terms(p + 1)], 0)
+        right = [jnp.concatenate([weight(n, 0), weight(n, 2)], 0) for n in (p, p + 1)]
+        both = jnp.dot(left, jnp.concatenate(right, 1), preferred_element_type=F32)
+        contrib[slab(p, FULL), :] = both[:FULL, :LANES]
+        contrib[slab(p + 1, FULL), :] = both[FULL:, LANES:]
+
+    def end_weights(p):
+        end_rows[pl.ds(p, 1), :] = weights[p, pl.ds(2 * LANES, 16), :].astype(F32)[0:1]
+        end_rows[pl.ds(LANES + p, 1), :] = weights[p, pl.ds(3 * LANES - 16, 16), :].astype(F32)[15:16]
+
+    for ref, start in ((end_rows, 0), (end_rows, LANES), (pair_rows, 0)):
+        ref[pl.ds(start + PAIRS, LANES - PAIRS), :] = jnp.zeros((LANES - PAIRS, LANES), F32)
+    loop(PAIRS, 8, end_weights)
+    landed_whole(0)
+    loop(PAIRS // 2, 7, upper_product)
 
     is_volume = small_row == VOLUME - FULL
     ones = jnp.ones((8, LANES), F32)
     blank = jnp.zeros((8, LANES), F32)
-    none = jnp.zeros((FULL, LANES), BF16)
-
-    def first_terms(p):
+
+    def lower_terms(p):
         e = slots[0, p]
-        second = lax.rem(e, 2) == 1
-        values = recv_a[e]
         low = recv_c[e // 2].astype(F32)
-        low = jnp.where(second, pltpu.roll(low, 4, 0), low)
-        wide = values.astype(F32)
-        ends = edge_tiles[e]
-        parts = [
-            grad_y(cells, ends[8 * n : 8 * n + 8])
-            for n, cells in enumerate((wide[0:8], wide[8:16], low))
-        ]
+        low = jnp.where(lax.rem(e, 2) == 1, pltpu.roll(low, 4, 0), low)
         low_u = jnp.where(is_volume, ones, low)
         low_g = jnp.where(is_volume, blank, pltpu.roll(low, 6, 0))
-        low_y = jnp.where(is_volume, blank, parts[2])
-        upper = jnp.concatenate([values, none, jnp.concatenate(parts[:2], 0).astype(BF16)], 1)
-        lower = jnp.concatenate([low_u, low_g, low_y], 1).astype(BF16)
-        return jnp.concatenate([upper, lower], 0)
-
-    def slab(p, size):
-        return pl.ds(pl.multiple_of(p * SLAB, SLAB), size)
-
-    def first_product(q):
+        low_y = jnp.where(is_volume, blank, grad_y(low))
+        return jnp.concatenate([low_u, low_g, low_y], 1)
+
+    def lower_product(q):
         p = 2 * q
-        left = jnp.concatenate([first_terms(p), first_terms(p + 1)], 0)
+        left = jnp.concatenate([lower_terms(p), lower_terms(p + 1)], 0).astype(BF16)
         right = jnp.concatenate([weights[p], weights[p + 1]], 1)
         both = jnp.dot(left, right, preferred_element_type=F32)
-        contrib[slab(p, SLAB), :] = both[:SLAB, :LANES]
-        contrib[slab(p + 1, SLAB), :] = both[SLAB:, LANES:]
-
-    loop(PAIRS // 2, 7, first_product)
-
-    chosen = (iota((ROWS, PAIRS), 0) == blocks[...]).astype(BF16)
+        contrib[slab(p, 8, FULL), :] = both[:8, :LANES]
+        contrib[slab(p + 1, 8, FULL), :] = both[8:, LANES:]
+
+    landed_whole(1)
+    loop(PAIRS // 2, 7, lower_product)
+
+    landed_whole(3)
+
+    def pair_row(p):
+        e = slots[0, p]
+        edges = recv_e[e // 2]
+        pair_rows[pl.ds(p, 1), :] = jnp.where(lax.rem(e, 2) == 1, pltpu.roll(edges, 64, 1), edges)
+
+    loop(PAIRS, 8, pair_row)
+    turned = pair_rows[...].T
+    chosen = (iota((ROWS, PAIRS), 0) == blocks[...]).astype(F32)
+    wide = jnp.concatenate([chosen, jnp.zeros((ROWS, LANES - PAIRS), F32)], 1)
+    chosen = chosen.astype(BF16)
+    for start in range(0, FIELDS, 6):
+        left = [
+            jnp.concatenate([wide * turned[f : f + 1], wide * turned[SLAB + f : SLAB + f + 1]], 1)
+            for f in range(start, start + 6)
+        ]
+        u[pl.ds(start * ROWS, 6 * ROWS), :] = jnp.dot(
+            jnp.concatenate(left, 0).astype(BF16),
+            end_rows[...].astype(BF16),
+            preferred_element_type=F32,
+        )
 
     def gathered(f):
         terms = contrib[pl.ds(f, PAIRS, stride=SLAB), :]
@@ -407,9 +424,9 @@
             chosen, low, preferred_element_type=F32
         )
 
-    volume[...] = gathered(VOLUME)
+    volume[...] = 1.0 / gathered(VOLUME)
     for f in range(FIELDS):
-        u[pl.ds(f * ROWS, ROWS), :] = gathered(f)
+        u[pl.ds(f * ROWS, ROWS), :] += gathered(f)
 
     landed_whole(2)
 
@@ -422,28 +439,32 @@
         contrib[slab(p, FULL), :] = both[:FULL, :LANES]
         contrib[slab(p + 1, FULL), :] = both[FULL:, LANES:]
 
-    loop(PAIRS // 2, 14, second_product)
+    loop(PAIRS // 2, PAIRS // 2, second_product)
 
     head, tail = zeros, zeros
     for f in range(FIELDS):
         cells = field(u, f)
         if f < FULL:
             cells = cells + gathered(f)
-        cells = cells / volume[...]
+        cells = cells * volume[...]
         u[pl.ds(f * ROWS, ROWS), :] = cells
-        head = jnp.where(lane == 2 * f, pltpu.roll(cells, 2 * f, 1) if f else cells, head)
-        tail = jnp.where(lane == 2 * f + 1, pltpu.roll(cells, 2 * f + 2, 1), tail)
 
     row_out2[0] = jnp.concatenate([u[pl.ds(ROWS - 1, SLAB, stride=ROWS), :], blank], 0).astype(BF16)
     row_out2[1] = jnp.concatenate([u[pl.ds(0, SLAB, stride=ROWS), :], blank], 0).astype(BF16)
-    col_out2[0] = tail.astype(BF16)
-    col_out2[1] = head.astype(BF16)
     halo = exchange(
         (row_out2.at[0], row_out2.at[1], col_out2.at[0], col_out2.at[1]),
         (row_in2.at[0], row_in2.at[1], col_in2.at[0], col_in2.at[1]),
         halo_send2,
         halo_recv2,
     )
+    start_exchange(halo, (0, 1))
+    for f in range(FIELDS):
+        cells = field(u, f)
+        head = jnp.where(lane == 2 * f, pltpu.roll(cells, 2 * f, 1) if f else cells, head)
+        tail = jnp.where(lane == 2 * f + 1, pltpu.roll(cells, 2 * f + 2, 1), tail)
+    col_out2[0] = tail.astype(BF16)
+    col_out2[1] = head.astype(BF16)
+    start_exchange(halo, (2, 3))
     ends = jnp.logical_or(lane == 0, lane == LANES - 1)
     for f in range(FIELDS):
         here = pl.ds(f * ROWS, ROWS)
@@ -520,8 +541,8 @@
             pltpu.VMEM((2 * count, 16, LANES), BF16),
             pltpu.VMEM((count, 8, LANES), BF16),
             pltpu.VMEM((count, 1, LANES), F32),
-            pltpu.VMEM((count, LANES), F32),
-            pltpu.VMEM((CAP * count, SLAB, LANES), F32),
+            pltpu.VMEM((2 * LANES, LANES), F32),
+            pltpu.VMEM((LANES, LANES), F32),
             pltpu.SMEM((1, CAP * count), jnp.int32),
             pltpu.SMEM((1, PAIRS), jnp.int32),
             pltpu.VMEM((1, PAIRS), jnp.int32),

time: 46.8 us -> 46.4 us (level)
  no operation moved by 1% of the time
where the time goes in v4:
time: 46.4 us; the launch traced here: 46.1 us
  Pallas kernels  45.5 us (98%)
  between operations  0.64 us (1%)
    pallas_call x1, Pallas kernels, shards(): pl.pallas_call(functools.partial(kernel, nx, ny), out_shape=(jax.ShapeDty...  44.4 us
    pallas_call x1, Pallas kernels, shards(): pl.pallas_call(finish, out_shape=(jax.ShapeDtypeStruct(flat, F32), jax.Sh...  1.03 us

profile of v4, /device:TPU:1, one launch (start us, length us, event | category | flops | bytes accessed | tf_op | source)
XLA Modules:
  0.0 46.1 jit_solution(14818471371008714353)
XLA Ops:
  0.6 44.4 %shard_map.77 = (f32[1152,128]{1,0:T(8,128)S(1)}, f32[1152,128]{1,0:T(8,128)S(1)}) custom-call(f32[1152,128]{1,0:T(8,128)} %bitcast.5, bf16[112,384,128]{2,1,0:T(8,128)(2,1)} %bitcast.4, s32[1,256]{1,0:T(1,128)} %wanted_hbm.1, s32[1,112]{1,0:T(1,128)} %slots_hbm.1, s32[1,112]{1,0:T(1,128)} %blocks_hbm.1, f32[18]{0:T(128)} %kappa_hbm.1), custom_call_target="tpu_custom_call" | custom-call | flops 264241152 | bytes 12582912 | tf_op jit(solution)/shard_map/pallas_call | solution.py:519
  45.1 1.0 %shard_map.78 = (f32[1152,128]{1,0:T(8,128)}, f32[1152,128]{1,0:T(8,128)}) custom-call(f32[1152,128]{1,0:T(8,128)S(1)} %get-tuple-element.6.cells, f32[1152,128]{1,0:T(8,128)S(1)} %get-tuple-element.7.flux), custom_call_target="tpu_custom_call" | custom-call | tf_op jit(solution)/shard_map/pallas_call | solution.py:585

commit v5 on v4

--- a/solution.py
+++ b/solution.py
@@ -19,6 +19,7 @@
 CAP = 2
 SLAB = 24
 VOLUME = 18
+PIECES = 6
 
 
 def chip_offsets():
@@ -144,7 +145,8 @@
         def _():
             pl.semaphore_signal(barrier, inc=1, device_id=(di, dj), device_id_type=MESH)
 
-    lax.fori_loop(0, nx, greet, 0)
+    for k in range(nx):
+        greet(k, 0)
 
     after_x = (lax.rem(i + 1, nx), j)
     before_x = (lax.rem(i + nx - 1, nx), j)
@@ -167,17 +169,21 @@
     get_old.wait()
     row_out[0] = u[pl.ds(ROWS - 1, SLAB, stride=ROWS), :]
     row_out[1] = u[pl.ds(0, SLAB, stride=ROWS), :]
-    columns = [zeros] * 4
-    for f in range(FIELDS):
-        cells = field(u, f)
-        for n, back in enumerate((0, 1, LANES - 2, LANES - 1)):
-            shift = (f - back) % LANES
-            moved = pltpu.roll(cells, shift, 1) if shift else cells
-            columns[n] = jnp.where(lane == f, moved, columns[n])
-    col_out[0] = columns[3]
-    col_out[1] = columns[0]
-    inner[0] = columns[1]
-    inner[1] = columns[2]
+
+    def columns(*places):
+        found = [zeros] * len(places)
+        for f in range(FIELDS):
+            cells = field(u, f)
+            for n, place in enumerate(places):
+                shift = (f - place) % LANES
+                moved = pltpu.roll(cells, shift, 1) if shift else cells
+                found[n] = jnp.where(lane == f, moved, found[n])
+        return found
+
+    head, tail = columns(0, LANES - 1)
+    col_out[0] = tail.astype(BF16)
+    col_out[1] = head.astype(BF16)
+    inner[2], inner[3] = head, tail
 
     def value_row(r):
         table_u[r] = u[pl.ds(r, FULL, stride=ROWS), :].astype(BF16)
@@ -270,6 +276,8 @@
     small[0].wait()
     send((0, 2, pack_a, send_a, recv_a), together=False)
 
+    inner[0], inner[1] = columns(1, LANES - 2)
+
     exchanged(halo)
     for f in range(FIELDS):
         cells = field(u, f)
@@ -283,9 +291,9 @@
             rest[pl.ds((f - FULL) * ROWS, ROWS), :] = cells
             rest[pl.ds((2 + f - FULL) * ROWS, ROWS), :] = grad
 
-    head, tail = col_out[1], col_out[0]
-    west = jnp.where(first_y, head, col_in[0])
-    east = jnp.where(last_y, tail, col_in[1])
+    head, tail = inner[2], inner[3]
+    west = jnp.where(first_y, head, col_in[0].astype(F32))
+    east = jnp.where(last_y, tail, col_in[1].astype(F32))
     edges = minmod(inner[0] - head, head - west)
     edges = jnp.where(
         lane < SLAB, edges, pltpu.roll(minmod(east - tail, tail - inner[1]), SLAB, 1)
@@ -318,7 +326,7 @@
         ref[2 * at] = table_g[row_of(d, 0)]
         ref[2 * at + 1] = table_g[row_of(d, 1)]
 
-    send((2, 2, pack_b, send_b, recv_b))
+    send((2, 2, pack_b, send_b, recv_b), together=False)
 
     for copy in small[1:]:
         copy.wait()
@@ -498,10 +506,13 @@
 
 
 def finish(cells, flux, cells_out, flux_out, sem):
-    copies = [
-        pltpu.make_async_copy(cells, cells_out, sem.at[0]),
-        pltpu.make_async_copy(flux, flux_out, sem.at[1]),
-    ]
+    copies = []
+    for source, target in ((cells, cells_out), (flux, flux_out)):
+        for n in range(PIECES):
+            part = pl.ds(n * FIELDS * ROWS // PIECES, FIELDS * ROWS // PIECES)
+            copies.append(
+                pltpu.make_async_copy(source.at[part], target.at[part], sem.at[len(copies)])
+            )
     for copy in copies:
         copy.start()
     for copy in copies:
@@ -527,7 +538,7 @@
         scratch_shapes=[
             pltpu.VMEM(padded, F32),
             pltpu.VMEM(flat, F32),
-            pltpu.VMEM((2, ROWS, LANES), F32),
+            pltpu.VMEM((4, ROWS, LANES), F32),
             pltpu.VMEM((8 * ROWS, LANES), F32),
             pltpu.VMEM((ROWS, FULL, LANES), BF16),
             pltpu.VMEM((ROWS, FULL, LANES), BF16),
@@ -552,8 +563,8 @@
             pltpu.VMEM((ROWS, LANES), F32),
             pltpu.VMEM((2, SLAB, LANES), F32),
             pltpu.VMEM((2, SLAB, LANES), F32),
-            pltpu.VMEM((2, ROWS, LANES), F32),
-            pltpu.VMEM((2, ROWS, LANES), F32),
+            pltpu.VMEM((2, ROWS, LANES), BF16),
+            pltpu.VMEM((2, ROWS, LANES), BF16),
             pltpu.VMEM((2, 32, LANES), BF16),
             pltpu.VMEM((2, 32, LANES), BF16),
             pltpu.VMEM((2, ROWS, LANES), BF16),
@@ -587,7 +598,7 @@
         out_shape=(jax.ShapeDtypeStruct(flat, F32), jax.ShapeDtypeStruct(flat, F32)),
         in_specs=[vmem, vmem],
         out_specs=(hbm, hbm),
-        scratch_shapes=[pltpu.SemaphoreType.DMA((2,))],
+        scratch_shapes=[pltpu.SemaphoreType.DMA((2 * PIECES,))],
         compiler_params=pltpu.CompilerParams(vmem_limit_bytes=4 * 2**20),
     )(cells, fluxes)
     return new_fields.reshape(shape), flux.reshape(shape)

time: 46.4 us -> 45.8 us (0.987)
  no operation moved by 1% of the time
where the time goes in v5:
time: 45.8 us; the launch traced here: 45.7 us
  Pallas kernels  45.1 us (98%)
  between operations  0.64 us (1%)
    pallas_call x1, Pallas kernels, shards(): pl.pallas_call(functools.partial(kernel, nx, ny), out_shape=(jax.ShapeDty...  44 us
    pallas_call x1, Pallas kernels, shards(): pl.pallas_call(finish, out_shape=(jax.ShapeDtypeStruct(flat, F32), jax.Sh...  1.1 us

profile of v5, /device:TPU:1, one launch (start us, length us, event | category | flops | bytes accessed | tf_op | source)
XLA Modules:
  0.0 45.7 jit_solution(13107270969821941097)
XLA Ops:
  0.6 44.0 %shard_map.77 = (f32[1152,128]{1,0:T(8,128)S(1)}, f32[1152,128]{1,0:T(8,128)S(1)}) custom-call(f32[1152,128]{1,0:T(8,128)} %bitcast.5, bf16[112,384,128]{2,1,0:T(8,128)(2,1)} %bitcast.4, s32[1,256]{1,0:T(1,128)} %wanted_hbm.1, s32[1,112]{1,0:T(1,128)} %slots_hbm.1, s32[1,112]{1,0:T(1,128)} %blocks_hbm.1, f32[18]{0:T(128)} %kappa_hbm.1), custom_call_target="tpu_custom_call" | custom-call | flops 264241152 | bytes 12582912 | tf_op jit(solution)/shard_map/pallas_call | solution.py:530
  44.6 1.1 %shard_map.78 = (f32[1152,128]{1,0:T(8,128)}, f32[1152,128]{1,0:T(8,128)}) custom-call(f32[1152,128]{1,0:T(8,128)S(1)} %get-tuple-element.6.cells, f32[1152,128]{1,0:T(8,128)S(1)} %get-tuple-element.7.flux), custom_call_target="tpu_custom_call" | custom-call | tf_op jit(solution)/shard_map/pallas_call | solution.py:596
